TPU v7x, 512 devices: a whole 4x4x16 slice. The times are simulated.
512 devices in a mesh: tok: 16 (over x_hi, y, core), atom: 32 (over z, x_lo).
Axes of the slice: x: 4 (x_hi: 2, x_lo: 2; x = x_hi * 2 + x_lo), y: 4, z: 16, core: 2. Of those that a mesh axis runs over, the one named last changes fastest.
Arguments:
- atoms: bfloat16 [655360, 128], P(('tok', 'atom')), may hold values from -6 to 6
- atom_bias: bfloat16 [655360, 4, 128], P(('tok', 'atom')), may hold values from -400 to 400
- atom_token: int32 [655360], P(('tok', 'atom')), may hold values from 0 to 4095, as said below
- token_atoms: int32 [65536], P(('tok', 'atom')), may hold values from 1 to 1793, as said below
- token_single: bfloat16 [65536, 768], P(('tok', 'atom')), may hold values from -6 to 6
- key_value: bfloat16 [2, 64, 768], P(None, 'tok'), may hold values from -6 to 6
- pair: bfloat16 [65536, 64, 128], P(('tok', 'atom')), may hold values from -600 to 600
- atom_gain: float32 [128], replicated, may hold values from 0.1 to 1.9
- atom_qkv: bfloat16 [128, 384], replicated, may hold values from -0.5 to 0.5
- atom_out_weight: bfloat16 [128, 128], replicated, may hold values from -0.5 to 0.5
- agg_weight: bfloat16 [128, 768], replicated, may hold values from -0.5 to 0.5
- token_gain: float32 [768], replicated, may hold values from 0.1 to 1.9
- query_gate_weight: bfloat16 [2, 768, 768], P(None, None, 'tok'), may hold values from -0.625 to 0.625
- pair_weight: bfloat16 [128, 16], replicated, may hold values from -0.5 to 0.5
- out_weight: bfloat16 [768, 768], P('tok'), may hold values from -0.21875 to 0.21875
Outputs:
- atom_update: bfloat16 [655360, 128], P(('tok', 'atom'))
- token_update: bfloat16 [65536, 768], P(('tok', 'atom'))
Inputs may be any that keep to these rules, and one draw needn't show every extreme that they name: `atom_token`: within each group the atoms belong to the group's tokens in non-decreasing order, token u of the group having token_atoms of it atoms; atom r of a group belongs to a token u with |r // 1280 - u // 128| <= 1. `token_atoms`: the counts of a group sum to 40960.
All inputs are finite; a program needn't handle non-finite values.
Results may differ from a plain program's by a relative error of at most 0.014.
Values may be sent and summed in bfloat16 or wider, within the bound.
A program may use at most 64 MiB of HBM per device.

v0:
```python
import jax
import jax.numpy as jnp
from jax import lax
from jax.sharding import PartitionSpec as P

ATOM_HEADS = 4
C_TOKEN = 768
HEADS = 16
QWIN = 32
KWIN = 128
RIM = 48


EPSILON = 1e-05


def extended(block, sides, width):
    for axis, dim in sides:
        count = lax.axis_size(axis)
        forward = [(i, i + 1) for i in range(count - 1)]
        backward = [(target, source) for source, target in forward]
        low = lax.ppermute(
            lax.slice_in_dim(block, block.shape[dim] - width, None, axis=dim), axis, forward
        )
        high = lax.ppermute(lax.slice_in_dim(block, 0, width, axis=dim), axis, backward)
        block = jnp.concatenate([low, block, high], axis=dim)
    return block


def layer_norm(values, gain):
    centre = values - jnp.mean(values, axis=-1, keepdims=True)
    spread = jnp.mean(centre * centre, axis=-1, keepdims=True)
    return centre * lax.rsqrt(spread + EPSILON) * gain


def project_atoms(rows, atom_gain, atom_qkv):
    normed = layer_norm(rows.astype(jnp.float32), atom_gain).astype(jnp.bfloat16)
    return jnp.dot(normed, atom_qkv, preferred_element_type=jnp.float32).astype(jnp.bfloat16)


def atom_window(queries, padded, biases, valid, heads):
    windows = queries.shape[0] // QWIN
    width = queries.shape[1]
    head_size = width // heads
    span_blocks = KWIN // QWIN
    blocks = padded.reshape(windows + span_blocks - 1, QWIN, 2 * width)
    gathered = jnp.concatenate(
        [blocks[offset : offset + windows] for offset in range(span_blocks)], axis=1
    )
    query_heads = queries.reshape(windows, QWIN, heads, head_size)
    key_heads = gathered[:, :, :width].reshape(windows, KWIN, heads, head_size)
    value_heads = gathered[:, :, width:].reshape(windows, KWIN, heads, head_size)
    scores = jnp.einsum(
        "wqhd,wkhd->wqhk", query_heads, key_heads, preferred_element_type=jnp.float32
    ) * head_size ** (-0.5)
    scores = scores + biases.astype(jnp.float32).reshape(windows, QWIN, heads, KWIN)
    scores = jnp.where(valid[:, None, None, :], scores, -1e30)
    largest = jnp.max(scores, axis=-1, keepdims=True)
    weights = jnp.exp(scores - largest)
    totals = jnp.sum(weights, axis=-1)
    mixed = jnp.einsum(
        "wqhk,wkhd->wqhd",
        weights.astype(jnp.bfloat16),
        value_heads,
        preferred_element_type=jnp.float32,
    )
    mixed = mixed / totals[..., None]
    return mixed.reshape(windows * QWIN, width).astype(jnp.bfloat16)


def body(
    atoms,
    atom_bias,
    atom_token,
    token_atoms,
    token_single,
    key_value,
    pair,
    atom_gain,
    atom_qkv,
    atom_out_weight,
    agg_weight,
    token_gain,
    query_gate_weight,
    pair_weight,
    out_weight,
):
    atom_rows = atoms.shape[0]
    width = atoms.shape[1]
    atom_devices = lax.axis_size("atom")
    owner = lax.axis_index("atom")
    projected = project_atoms(atoms, atom_gain, atom_qkv)
    queries = projected[:, :width]
    padded = extended(projected[:, width:], (("atom", 0),), RIM)
    windows = atom_rows // QWIN
    positions = (
        owner * atom_rows - RIM + jnp.arange(windows)[:, None] * QWIN + jnp.arange(KWIN)[None, :]
    )
    valid = (positions >= 0) & (positions < atom_rows * atom_devices)
    mixed = atom_window(queries, padded, atom_bias, valid, ATOM_HEADS)
    updated = (
        atoms.astype(jnp.float32)
        + jnp.dot(mixed, atom_out_weight, preferred_element_type=jnp.float32)
    ).astype(jnp.bfloat16)
    lifted = jax.nn.relu(jnp.dot(updated, agg_weight, preferred_element_type=jnp.float32)).astype(
        jnp.bfloat16
    )
    tok_rows = token_single.shape[0]
    channels = token_single.shape[1]
    slots = atom_token - (owner - 1) * tok_rows
    onehot = (slots[None, :] == jnp.arange(3 * tok_rows)[:, None]).astype(jnp.bfloat16)
    partial_sums = jnp.dot(onehot, lifted, preferred_element_type=jnp.float32).reshape(
        3, tok_rows, channels
    )
    bordered = extended(partial_sums.astype(jnp.bfloat16), (("atom", 0),), 1).astype(
        partial_sums.dtype
    )
    sums = bordered[0] + bordered[2] + bordered[4]
    acts = sums / token_atoms.astype(jnp.float32)[:, None] + token_single.astype(jnp.float32)
    token_normed = layer_norm(acts, token_gain).astype(jnp.bfloat16)
    biases = jnp.einsum(
        "qkc,ch->qhk", pair, pair_weight, preferred_element_type=jnp.float32
    ).astype(jnp.bfloat16)
    head_size = C_TOKEN // HEADS
    scale = head_size ** (-0.5)
    both = jnp.einsum(
        "tc,gcn->gtn",
        token_normed,
        lax.all_gather(query_gate_weight, "tok", axis=2, tiled=True),
        preferred_element_type=jnp.float32,
    )
    query_heads = both[0].astype(jnp.bfloat16).reshape(tok_rows, HEADS, head_size)
    gates = jax.nn.sigmoid(both[1])
    piece = lax.all_gather(key_value, "tok", axis=1, tiled=True)
    largest = jnp.full((tok_rows, HEADS), -1e30, jnp.float32)
    count = piece.shape[1]
    key_heads = piece[0].reshape(count, HEADS, head_size)
    value_heads = piece[1].reshape(count, HEADS, head_size)
    scores = (
        jnp.einsum("qhd,khd->qhk", query_heads, key_heads, preferred_element_type=jnp.float32)
        * scale
    )
    scores = scores + biases.astype(jnp.float32)
    fresh = jnp.maximum(largest, jnp.max(scores, axis=-1))
    weights = jnp.exp(scores - fresh[..., None])
    totals = jnp.sum(weights, axis=-1)
    accum = jnp.einsum(
        "qhk,khd->qhd",
        weights.astype(jnp.bfloat16),
        value_heads,
        preferred_element_type=jnp.float32,
    )
    largest, totals, accum = (fresh, totals, accum)
    token_mixed = accum / totals[..., None]
    gated = (gates * token_mixed.reshape(tok_rows, channels)).astype(jnp.bfloat16)
    attended = jnp.dot(
        gated,
        lax.all_gather(out_weight, "tok", axis=0, tiled=True),
        preferred_element_type=jnp.float32,
    )
    token_update = (acts + attended).astype(jnp.bfloat16)
    return (updated, token_update)


def solution(mesh):
    return jax.shard_map(
        body,
        mesh=mesh,
        in_specs=(
            P(("tok", "atom"), None),
            P(("tok", "atom"), None, None),
            P(("tok", "atom")),
            P(("tok", "atom")),
            P(("tok", "atom"), None),
            P(None, "tok", None),
            P(("tok", "atom"), None, None),
            P(),
            P(),
            P(),
            P(),
            P(),
            P(None, None, "tok"),
            P(),
            P("tok", None),
        ),
        out_specs=(P(("tok", "atom"), None), P(("tok", "atom"), None)),
        check_vma=False,
    )
```

profile of v0, /device:TPU:1, one launch (start us, length us, event | category | flops | bytes accessed | tf_op | source)
XLA Modules:
  0.0 153.1 jit_solution(6369568160766683572)
XLA Ops:
  7.2 0.0 copy-start
  7.2 0.0 copy-start.8
  7.2 0.0 copy-start.9
  7.2 0.0 all-gather.3.cloned.1.call-start
  7.2 0.7 all-gather.3.cloned.1.call-update
  7.9 0.0 all-gather.5.cloned.1.call-start
  8.0 1.1 convert_reduce_fusion
  9.1 1.4 fusion.22
  10.6 1.6 %convolution_convert_fusion = bf16[1280,384]{1,0:T(8,128)(2,1)S(1)} fusion(bf16[128,384]{1,0:T(8,128)(2,1)} %param.23, bf16[1280,128]{1,0:T(8,128)(2,1)} %param.15, f32[128]{0:T(128)} %param.22, f32[1280]{0:T(1024)S(1)} %add_rsqrt_fusion, f32[1280]{0:T(1024)S(1)} %broadcast_multiply_fusion), kind=kOutput, calls=%fused_computation.2 | convolution fusion | flops 127139840 | bytes 1419776 | tf_op jit(solution)/shard_map/dot_general | solution.py:38
  12.2 3.9 %collective-permute-start = (bf16[48,256]{1,0:T(8,128)(2,1)S(1)}, bf16[48,256]{1,0:T(8,128)(2,1)S(1)}, u32[]{:S(2)}, u32[]{:S(2)}) collective-permute-start(bf16[48,256]{1,0:T(8,128)(2,1)S(1)} %get-tuple-element.6), channel_id=1, source_target_pairs={{0,1},{1,2},{2,3},{3,4},{4,5},{5,6},{6,7},{7,8},{8,9},{9,10},{10,1... | collective-permute-start | bytes 73736 | tf_op jit(solution)/shard_map/ppermute | solution.py:22
  16.1 1.3 collective-permute-start.1
  17.4 0.0 all-gather.5.cloned.1.call-update
  17.5 0.0 copy-done.8
  17.5 25.4 %all_gather.10 = bf16[2,64,768]{2,0,1:T(2,128)(2,1)S(1)} all-gather(bf16[2,4,768]{2,0,1:T(2,128)(2,1)S(1)} %copy.47), channel_id=1, replica_groups=mesh['tok'=16,'atom'=32] {'tok'}, dimensions={1}, use_global_device_ids=true | all-gather | bytes 208896 | tf_op jit(solution)/shard_map/all_gather | solution.py:134
  42.9 1.0 fusion.60
  43.9 0.0 copy-done.9
  43.9 0.1 fusion.52
  44.0 0.9 slice.108
  45.0 0.0 copy-start.12
  45.0 0.0 copy-start.3
  45.0 1.6 %reshape.115 = bf16[40,32,4,32]{3,2,1,0:T(4,128)(2,1)} reshape(bf16[1280,128]{1,0:T(8,128)(2,1)S(1)} %slice.115) | data formatting | bytes 655360 | tf_op jit(solution)/shard_map/reshape | solution.py:50
  46.6 2.6 %copy.43 = bf16[1280,4,128]{2,0,1:T(8,128)(2,1)} copy(bf16[1280,4,128]{2,1,0:T(4,128)(2,1)} %param.16) | data formatting | bytes 2621440 | tf_op args[1]
  49.2 0.0 copy-done.12
  49.2 0.0 copy-done.4
  49.2 0.9 copy.51
  50.1 0.0 copy-done.3
  50.1 0.9 copy.48
  51.0 0.0 collective-permute-done
  51.0 0.0 collective-permute-done.1
  51.0 0.0 copy-done.1
  51.0 0.2 fusion.21
  51.2 0.3 pad_maximum_fusion
  51.5 1.8 %fusion.58 = (bf16[40,128,128]{2,1,0:T(8,128)(2,1)S(1)}, bf16[40,128,128]{2,1,0:T(8,128)(2,1)}) fusion(bf16[40,128,256]{2,1,0:T(8,128)(2,1)S(1)} %pad_maximum_fusion), kind=kLoop, calls=%fused_computation.91 | loop fusion | bytes 5242880 | tf_op jit(solution)/shard_map/slice | solution.py:51
  53.3 2.4 %copy.39 = bf16[40,128,128]{1,2,0:T(8,128)(2,1)} copy(bf16[40,128,128]{2,1,0:T(8,128)(2,1)} %get-tuple-element.5) | data formatting | bytes 2621440 | tf_op jit(solution)/shard_map/slice | solution.py:52
  55.7 1.4 copy.40
  57.1 3.1 %fusion.61 = (f32[40,32,4]{1,2,0:T(4,128)S(1)}, f32[40,32,4,128]{3,1,2,0:T(8,128)S(1)}) fusion(bf16[40,128,4,32]{1,3,2,0:T(8,128)(2,1)} %bitcast.70, bf16[40,32,4,32]{3,2,1,0:T(4,128)(2,1)} %reshape.115, pred[40,128]{1,0:T(8,128)(4,1)S(1)} %fusion.52, bf16[40,32,4,128]{3,1,0,2:T(8,128)(2,1)} %bitcast.69), kind=kOutput, calls=%fused_computation.94 | convolution fusion | flops 45214720 | bytes 5596160 | tf_op jit(solution)/shard_map/wqhd,wkhd->wqhk/dot_general | solution.py:53
  60.2 1.6 %fusion.4 = f32[40,32,4]{1,2,0:T(4,128)S(1)} fusion(f32[40,32,4,128]{3,1,2,0:T(8,128)S(1)} %get-tuple-element.19, f32[40,32,4]{1,2,0:T(4,128)S(1)} %get-tuple-element.18), kind=kLoop, calls=%fused_computation.11 | loop fusion | flops 1305600 | bytes 2662400 | tf_op jit(solution)/shard_map/reduce_sum | solution.py:60
  61.9 1.1 fusion.1
  63.0 0.0 copy-start.7
  63.0 0.8 copy.45
  63.9 1.5 %convert_element_type.72 = bf16[1280,128]{0,1:T(8,128)(2,1)} reshape(bf16[40,32,4,32]{1,0,3,2:T(8,128)(2,1)S(1)} %copy.45) | data formatting | bytes 655360 | tf_op jit(solution)/shard_map/convert_element_type | solution.py:68
  65.4 1.3 fusion.3
  66.8 0.0 copy-start.5
  66.8 0.0 copy-start.10
  66.8 2.5 %fusion.9 = bf16[384,768]{1,0:T(8,128)(2,1)S(1)} fusion(bf16[1280,128]{1,0:T(8,128)(2,1)S(1)} %fusion.3, bf16[128,768]{1,0:T(8,128)(2,1)} %param.25, s32[1280]{0:T(1024)S(1)} %broadcast_subtract_fusion), kind=kOutput, calls=%fused_computation.17 | convolution fusion | flops 1009385472 | bytes 1119232 | tf_op jit(solution)/shard_map/dot_general | solution.py:112
  69.3 0.0 copy-start.6
  69.3 1.4 collective-permute-start.3
  70.8 0.0 copy-start.11
  70.8 4.8 %collective-permute-start.2 = (bf16[1,128,768]{2,1,0:T(8,128)(2,1)S(1)}, bf16[1,128,768]{2,1,0:T(8,128)(2,1)S(1)}, u32[]{:S(2)}, u32[]{:S(2)}) collective-permute-start(bf16[1,128,768]{2,1,0:T(8,128)(2,1)S(1)} %get-tuple-element.14), channel_id=1, source_target_pairs={{0,1},{1,2},{2,3},{3,4},{4,5},{5,6},{6,7},{7,8},{8,9},{9,10},{10,1... | collective-permute-start | bytes 589832 | tf_op jit(solution)/shard_map/ppermute | solution.py:22
  75.6 1.2 fusion.6
  76.8 1.7 %collective-permute-done.3 = bf16[1,128,768]{2,1,0:T(8,128)(2,1)S(1)} collective-permute-done((bf16[1,128,768]{2,1,0:T(8,128)(2,1)S(1)}, bf16[1,128,768]{2,1,0:T(8,128)(2,1)S(1)}, u32[]{:S(2)}, u32[]{:S(2)}) %collective-permute-start.3) | collective-permute-done | bytes 196640 | tf_op jit(solution)/shard_map/ppermute | solution.py:25
  78.5 5.5 %collective-permute-done.2 = bf16[1,128,768]{2,1,0:T(8,128)(2,1)S(1)} collective-permute-done((bf16[1,128,768]{2,1,0:T(8,128)(2,1)S(1)}, bf16[1,128,768]{2,1,0:T(8,128)(2,1)S(1)}, u32[]{:S(2)}, u32[]{:S(2)}) %collective-permute-start.2) | collective-permute-done | bytes 196640 | tf_op jit(solution)/shard_map/ppermute | solution.py:22
  84.0 0.2 fusion.56
  84.3 0.2 multiply_reduce_fusion
  84.5 0.0 all-gather.3.cloned.1.call-done
  84.5 2.6 %convolution_bitcast_fusion = f32[2,128,768]{2,1,0:T(8,128)S(1)} fusion(bf16[2,768,768]{1,2,0:T(8,128)(2,1)} %all-gather.3.cloned.1.call-done, f32[128,768]{1,0:T(8,128)S(1)} %get-tuple-element.3, f32[768]{0:T(1024)S(1)} %copy-done.11, f32[128]{0:T(128)S(1)} %add_rsqrt_fusion.1, f32[128]{0:T(128)S(1)} %broadcast_multiply_fusion.1), kind=kOutput, calls=%fused_computation.20 | convolution fusion | flops 302383104 | bytes 3543040 | tf_op jit(solution)/shard_map/tc,gcn->gtn/dot_general | solution.py:126
  87.1 0.7 slice.152
  87.8 1.7 %copy.46 = bf16[1,128,768]{1,2,0:T(8,128)(2,1)} copy(bf16[1,128,768]{2,1,0:T(8,128)(2,1)} %slice.152) | data formatting | bytes 393216 | tf_op jit(solution)/shard_map/slice | solution.py:132
  89.5 1.3 fusion.62
  90.9 0.1 fusion.25
  91.0 1.9 %fusion.15 = f32[128,16,48]{0,2,1:T(8,128)} fusion(bf16[64,16,48]{0,2,1:T(8,128)(2,1)} %bitcast.80, f32[128,16,64]{0,2,1:T(8,128)S(1)} %get-tuple-element.21, f32[128,16]{0,1:T(8,128)S(1)} %broadcast_maximum_fusion, f32[128,16]{0,1:T(8,128)S(1)} %fusion.25), kind=kOutput, calls=%fused_computation.26 | convolution fusion | flops 12943360 | bytes 1032192 | tf_op jit(solution)/shard_map/qhk,khd->qhd/dot_general | solution.py:147
  92.9 1.9 %copy.52 = f32[128,768]{1,0:T(8,128)} copy(f32[128,768]{0,1:T(8,128)} %bitcast.79) | data formatting | bytes 786432 | tf_op jit(solution)/shard_map/reshape | solution.py:155
  94.8 49.1 %all-gather.5.cloned.1.call-done = bf16[768,768]{1,0:T(8,128)(2,1)} async-done(((bf16[48,768]{1,0:T(8,128)(2,1)}), bf16[768,768]{1,0:T(8,128)(2,1)}) %all-gather.5.cloned.1.call-update) | async-done | bytes 1179664 | tf_op jit(solution)/shard_map/all_gather | solution.py:158
  143.9 2.4 %fusion.16 = bf16[128,768]{1,0:T(8,128)(2,1)} fusion(f32[128,768]{1,0:T(8,128)S(1)} %get-tuple-element.3, bf16[768,768]{1,0:T(8,128)(2,1)} %all-gather.5.cloned.1.call-done, f32[128,768]{1,0:T(8,128)} %copy.52, f32[2,128,768]{2,1,0:T(8,128)S(1)} %convolution_bitcast_fusion), kind=kOutput, calls=%fused_computation.27 | convolution fusion | flops 151683072 | bytes 2555904 | tf_op jit(solution)/shard_map/dot_general | solution.py:156
  (22 shorter events, 0.1 us)
Async XLA Ops:
  7.2 68.4 %copy-start = (bf16[128,64,128]{2,1,0:T(8,128)(2,1)S(1)}, bf16[128,64,128]{2,1,0:T(8,128)(2,1)}, u32[]{:S(2)}) copy-start(bf16[128,64,128]{2,1,0:T(8,128)(2,1)} %param.21) | copy-start | bytes 6291460
  7.2 10.3 %copy-start.8 = (bf16[2,4,768]{2,1,0:T(4,128)(2,1)S(1)}, bf16[2,4,768]{2,1,0:T(4,128)(2,1)}, u32[]{:S(2)}) copy-start(bf16[2,4,768]{2,1,0:T(4,128)(2,1)} %param.20) | copy-start | bytes 36868
  7.2 36.8 %copy-start.9 = (s32[1280]{0:T(1024)S(1)}, s32[1280]{0:T(1024)}, u32[]{:S(2)}) copy-start(s32[1280]{0:T(1024)} %param.17) | copy-start | bytes 15364
  7.2 77.3 %all-gather.3.cloned.1.call-start = ((), (), s32[]{:S(2)}) async-start(), calls=%async_computation | async-start | bytes 2506752 | tf_op jit(solution)/shard_map/all_gather | solution.py:129
  7.9 135.9 %all-gather.5.cloned.1.call-start = ((), (), s32[]{:S(2)}) async-start(), calls=%async_computation.1 | async-start | bytes 1253376 | tf_op jit(solution)/shard_map/all_gather | solution.py:158
  12.2 38.8 %collective-permute-start = (bf16[48,256]{1,0:T(8,128)(2,1)S(1)}, bf16[48,256]{1,0:T(8,128)(2,1)S(1)}, u32[]{:S(2)}, u32[]{:S(2)}) collective-permute-start(bf16[48,256]{1,0:T(8,128)(2,1)S(1)} %get-tuple-element.6), channel_id=1, source_target_pairs={{0,1},{1,2},{2,3},{3,4},{4,5},{5,6},{6,7},{7,8},{8,9},{9,10},{10,1... | collective-permute-start | bytes 73736 | tf_op jit(solution)/shard_map/ppermute | solution.py:22
  16.1 34.9 %collective-permute-start.1 = (bf16[48,256]{1,0:T(8,128)(2,1)S(1)}, bf16[48,256]{1,0:T(8,128)(2,1)S(1)}, u32[]{:S(2)}, u32[]{:S(2)}) collective-permute-start(bf16[48,256]{1,0:T(8,128)(2,1)S(1)} %get-tuple-element.7), channel_id=1, source_target_pairs={{1,0},{2,1},{3,2},{4,3},{5,4},{6,5},{7,6},{8,7},{9,8},{10,9},{11,1... | collective-permute-start | bytes 73736 | tf_op jit(solution)/shard_map/ppermute | solution.py:25
  45.0 4.3 %copy-start.12 = (s32[128]{0:T(128)S(1)}, s32[128]{0:T(128)}, u32[]{:S(2)}) copy-start(s32[128]{0:T(128)} %param.18) | copy-start | bytes 1540
  45.0 5.2 %copy-start.3 = (bf16[1,64,768]{2,0,1:T(2,128)(2,1)S(1)}, bf16[1,64,768]{2,0,1:T(2,128)(2,1)}, u32[]{:S(2)}) copy-start(bf16[1,64,768]{2,0,1:T(2,128)(2,1)} %get-tuple-element.16) | copy-start | bytes 294916
  46.6 2.7 %copy-start.4 = (bf16[1,64,768]{2,0,1:T(2,128)(2,1)S(1)}, bf16[1,64,768]{2,0,1:T(2,128)(2,1)}, u32[]{:S(2)}) copy-start(bf16[1,64,768]{2,0,1:T(2,128)(2,1)} %get-tuple-element.17) | copy-start | bytes 294916
  46.6 4.4 %copy-start.1 = (bf16[1280,256]{1,0:T(8,128)(2,1)S(1)}, bf16[1280,256]{1,0:T(8,128)(2,1)}, u32[]{:S(2)}) copy-start(bf16[1280,256]{1,0:T(8,128)(2,1)} %slice.108) | copy-start | bytes 1966084
  60.2 1.7 %copy-start.2 = (bf16[40,128,128]{1,2,0:T(8,128)(2,1)S(1)}, bf16[40,128,128]{1,2,0:T(8,128)(2,1)}, u32[]{:S(2)}) copy-start(bf16[40,128,128]{1,2,0:T(8,128)(2,1)} %copy.39) | copy-start | bytes 3932164
  63.0 2.4 %copy-start.7 = (bf16[128,128]{1,0:T(8,128)(2,1)S(1)}, bf16[128,128]{1,0:T(8,128)(2,1)}, u32[]{:S(2)}) copy-start(bf16[128,128]{1,0:T(8,128)(2,1)} %param.24) | copy-start | bytes 98308
  66.8 2.5 %copy-start.5 = (bf16[1280,128]{1,0:T(8,128)(2,1)}, bf16[1280,128]{1,0:T(8,128)(2,1)S(1)}, u32[]{:S(2)}) copy-start(bf16[1280,128]{1,0:T(8,128)(2,1)S(1)} %fusion.3) | copy-start | bytes 983044
  66.8 8.8 %copy-start.10 = (bf16[128,16]{0,1:T(8,128)(2,1)S(1)}, bf16[128,16]{0,1:T(8,128)(2,1)}, u32[]{:S(2)}) copy-start(bf16[128,16]{0,1:T(8,128)(2,1)} %param.28) | copy-start | bytes 12292
  69.3 14.8 %copy-start.6 = (bf16[128,768]{1,0:T(8,128)(2,1)S(1)}, bf16[128,768]{1,0:T(8,128)(2,1)}, u32[]{:S(2)}) copy-start(bf16[128,768]{1,0:T(8,128)(2,1)} %param.19) | copy-start | bytes 589828
  69.3 9.2 %collective-permute-start.3 = (bf16[1,128,768]{2,1,0:T(8,128)(2,1)S(1)}, bf16[1,128,768]{2,1,0:T(8,128)(2,1)S(1)}, u32[]{:S(2)}, u32[]{:S(2)}) collective-permute-start(bf16[1,128,768]{2,1,0:T(8,128)(2,1)S(1)} %get-tuple-element.15), channel_id=1, source_target_pairs={{1,0},{2,1},{3,2},{4,3},{5,4},{6,5},{7,6},{8,7},{9,8},{10,9},{11,1... | collective-permute-start | bytes 589832 | tf_op jit(solution)/shard_map/ppermute | solution.py:25
  70.8 13.7 %copy-start.11 = (f32[768]{0:T(1024)S(1)}, f32[768]{0:T(1024)}, u32[]{:S(2)}) copy-start(f32[768]{0:T(1024)} %param.26) | copy-start | bytes 9220
  70.8 13.3 %collective-permute-start.2 = (bf16[1,128,768]{2,1,0:T(8,128)(2,1)S(1)}, bf16[1,128,768]{2,1,0:T(8,128)(2,1)S(1)}, u32[]{:S(2)}, u32[]{:S(2)}) collective-permute-start(bf16[1,128,768]{2,1,0:T(8,128)(2,1)S(1)} %get-tuple-element.14), channel_id=1, source_target_pairs={{0,1},{1,2},{2,3},{3,4},{4,5},{5,6},{6,7},{7,8},{8,9},{9,10},{10,1... | collective-permute-start | bytes 589832 | tf_op jit(solution)/shard_map/ppermute | solution.py:22
Sparse Core Ops, SparseCore 0:
  11.4 69.5 all-gather.2
  84.4 59.4 all-gather.4
where the time goes:
time: 154 us; the launch traced here: 153 us
  waiting for transfers between devices  57 us (37%)
  blocking collectives  25.4 us (16%)
  local copies, waits for them, and re-layouts  20.5 us (13%)
  matrix products  19.1 us (12%)
  between operations  14.4 us (9%)
  starting transfers between devices  11.5 us (7%)
  other arithmetic  5.24 us (3%)
    all_gather x1, waiting for transfers between devices, body(): lax.all_gather(out_weight, 'tok', axis=0, tiled=True)  49.1 us
    all_gather x1, blocking collectives, body(): piece = lax.all_gather(key_value, 'tok', axis=1, tiled=True)  25.4 us
    ppermute x2, starting transfers between devices, extended(): lax.ppermute(lax.slice_in_dim(block, block.shape[dim] - width, None, axis...  8.74 us
    ppermute x2, waiting for transfers between devices, extended(): lax.ppermute(lax.slice_in_dim(block, block.shape[dim] - width, None, axis...  5.54 us
    slice x2, local copies, waits for them, and re-layouts, atom_window(): key_heads = gathered[:, :, :width].reshape(windows, KWIN, heads, head_size)  3.24 us
  transfers between devices with their start and end apart: 6, of which 3 were waited for; matrix products, arithmetic and copies ran while one was open for 28% of the time, Pallas kernels for 0%

commit v1 on v0

v1 whole, which is shorter than its diff:
```python
import functools

import jax
import jax.numpy as jnp
from jax import lax
from jax.experimental import pallas as pl
from jax.experimental.pallas import tpu as pltpu
from jax.sharding import PartitionSpec as P

MESH = pl.DeviceIdType.MESH
F32 = jnp.float32
BF16 = jnp.bfloat16

ATOM_HEADS = 4
QWIN = 32
KWIN = 128
RIM = 48
ROWS = 1280
PADDED = ROWS + 2 * RIM
WIDTH = 128
TOK = 128
CH = 768
HEADS = 16
HEAD = 48
KEYS = 64
CHUNKS = 3
CHUNK = CH // CHUNKS
EPSILON = 1e-05
NT = (((1,), (1,)), ((), ()))


def mm(a, b):
    return jnp.dot(a, b, preferred_element_type=F32)


def mm_nt(a, b):
    return lax.dot_general(a, b, NT, preferred_element_type=F32)


def iota(shape, axis):
    return lax.broadcasted_iota(jnp.int32, shape, axis)


def layer_norm(values, gain):
    centre = values - jnp.mean(values, axis=-1, keepdims=True)
    spread = jnp.mean(centre * centre, axis=-1, keepdims=True)
    return centre * lax.rsqrt(spread + EPSILON) * gain


def kernel(
    comm,
    atoms_hbm,
    bias_hbm,
    slot_ref,
    count_ref,
    single_hbm,
    kv_ref,
    pair_hbm,
    atom_gain_ref,
    qkv_ref,
    atom_out_ref,
    agg_ref,
    token_gain_ref,
    qg_hbm,
    pair_weight_ref,
    out_hbm,
    atom_update_hbm,
    token_update_hbm,
    ap,
    bias,
    single,
    pair,
    qs,
    ks,
    vs,
    mx,
    up,
    oh,
    lf,
    own_sum,
    sb,
    rb,
    wq,
    wo,
    kv,
    raw,
    tb,
    kbd,
    vbd,
    mbd,
    acts,
    tu,
    local_sem,
    halo_send,
    halo_recv,
    w_send,
    w_recv,
    o_send,
    o_recv,
    k_send,
    k_recv,
    x_send,
    x_recv,
):
    if comm:
        tok = lax.axis_index("tok")
        me = lax.axis_index("atom")
    else:
        tok = jnp.int32(5)
        me = jnp.int32(7)
    core = lax.rem(tok, 2)
    row = lax.rem(lax.div(tok, 2), 4)
    hi = lax.div(tok, 8)
    lo = lax.rem(me, 2)
    left = lax.rem(me + 31, 32)
    right = lax.rem(me + 1, 32)
    twin = tok + 1 - 2 * core

    def place(flip, step, who):
        high = 1 - hi if flip else hi
        return (high * 4 + lax.rem(row + step + 4, 4)) * 2 + who

    def target(r):
        flip, step = divmod(r, 4)
        return (place(flip, step, core), me + 1 - 2 * lo if flip else me)

    def origin(r, who):
        flip, step = divmod(r, 4)
        return place(flip, -step, who)

    peers = [target(r) for r in range(1, 8)] + [(twin, me), (tok, left), (tok, right)]
    if comm:
        barrier = pltpu.get_barrier_semaphore()
        for peer in peers:
            pl.semaphore_signal(barrier, inc=1, device_id=peer, device_id_type=MESH)

    def local(i, src, dst):
        copy = pltpu.make_async_copy(src, dst, local_sem.at[i])
        copy.start()
        return copy

    def block(which):
        return pl.ds(pl.multiple_of(which * HEAD, 16), HEAD)

    atoms_in = local(0, atoms_hbm, ap.at[pl.ds(RIM, ROWS)])
    out_in = local(1, out_hbm, wo.at[block(tok)])
    bias_in = local(2, bias_hbm, bias)
    pair_in = local(3, pair_hbm, pair)
    single_in = local(4, single_hbm, single)

    qg_in = local(7, qg_hbm, wq.at[:, block(tok), :])
    kv[tok, 0:4, :] = kv_ref[0].astype(F32)
    kv[tok, 4:8, :] = kv_ref[1].astype(F32)

    def send(src, dst, ssem, rsem, device):
        return pltpu.make_async_remote_copy(
            src_ref=src, dst_ref=dst, send_sem=ssem, recv_sem=rsem,
            device_id=device, device_id_type=MESH,
        )

    def w_copy(which, i, device):
        ref = wq.at[:, block(which), :]
        return send(ref, ref, w_send.at[i], w_recv.at[i], device)

    def o_copy(which, i, device):
        ref = wo.at[block(which)]
        return send(ref, ref, o_send.at[i], o_recv.at[i], device)

    def k_copy(which, i, device):
        ref = kv.at[which]
        return send(ref, ref, k_send.at[i], k_recv.at[i], device)

    def halo_copy(side):
        if side == 0:
            src, dst, device = pl.ds(ROWS, RIM), pl.ds(0, RIM), (tok, right)
        else:
            src, dst, device = pl.ds(RIM, RIM), pl.ds(ROWS + RIM, RIM), (tok, left)
        return send(ap.at[src], ap.at[dst], halo_send.at[side], halo_recv.at[side], device)

    sends = []

    def go(copy):
        copy.start()
        sends.append(copy)

    atoms_in.wait()
    out_in.wait()
    qg_in.wait()
    if comm:
        pl.semaphore_wait(barrier, len(peers))
        for side in range(2):
            go(halo_copy(side))
        for r in range(1, 8):
            go(k_copy(tok, r, target(r)))
        for r in range(1, 8):
            go(w_copy(tok, r, target(r)))
        for r in range(1, 8):
            go(o_copy(tok, r, target(r)))
        go(k_copy(tok, 8, (twin, me)))
        go(w_copy(tok, 8, (twin, me)))
        go(o_copy(tok, 8, (twin, me)))

    def forward(copy, r):
        if comm:
            copy(origin(r, core), r, (twin, me)).wait_recv()
            go(copy(origin(r, core), 8 + r, (twin, me)))

    def arrive(copy, r):
        if comm:
            copy(origin(r, 1 - core), 8 + r, (twin, me)).wait_recv()

    def project(start, count, with_queries):
        values = ap[pl.ds(start, count), :].astype(F32)
        normed = layer_norm(values, atom_gain_ref[...]).astype(BF16)
        projected = mm(normed, qkv_ref[...]).astype(BF16)
        if with_queries:
            qs[pl.ds(start - RIM, count), :] = projected[:, :WIDTH]
        ks[pl.ds(start, count), :] = projected[:, WIDTH : 2 * WIDTH]
        vs[pl.ds(start, count), 0:WIDTH] = projected[:, 2 * WIDTH :]
        vs[pl.ds(start, count), WIDTH : 2 * WIDTH] = jnp.ones((count, WIDTH), BF16)

    for part in range(5):
        project(RIM + part * 256, 256, True)

    lane = iota((QWIN, WIDTH), 1)
    head_of_lane = lax.div(lane, 32)
    head_masks = [(head_of_lane == h).astype(F32).astype(BF16) for h in range(ATOM_HEADS)]
    mix_row = iota((KWIN, KWIN), 0)
    mix_col = iota((KWIN, KWIN), 1)
    source = lax.rem(mix_row, QWIN) * ATOM_HEADS + lax.div(mix_row, QWIN)
    reorder = (mix_col == source).astype(F32).astype(BF16)
    scale = 32 ** (-0.5)
    low_end = jnp.where(me == 0, RIM, 0)
    high_end = jnp.where(me == 31, ROWS + RIM, PADDED)

    def window(start, edge):
        queries = qs[pl.ds(start, QWIN), :]
        expanded = jnp.concatenate([queries * mask for mask in head_masks], axis=0)
        scores = mm_nt(expanded, ks[pl.ds(start, KWIN), :]) * scale
        scores += mm(reorder, bias[pl.ds(start * ATOM_HEADS, KWIN), :])
        if edge:
            place_of_key = start + mix_col
            inside = (place_of_key >= low_end) & (place_of_key < high_end)
            scores = jnp.where(inside, scores, -1e30)
        largest = jnp.max(scores, axis=1, keepdims=True)
        weights = jnp.exp(scores - largest).astype(BF16)
        both = mm(weights, vs[pl.ds(start, KWIN), :])
        rows = [both[h * QWIN : (h + 1) * QWIN] for h in range(ATOM_HEADS)]
        mixed, totals = rows[0][:, :WIDTH], rows[0][:, WIDTH:]
        for h in range(1, ATOM_HEADS):
            mixed = jnp.where(head_of_lane == h, rows[h][:, :WIDTH], mixed)
            totals = jnp.where(head_of_lane == h, rows[h][:, WIDTH:], totals)
        mx[pl.ds(start, QWIN), :] = (mixed / totals).astype(BF16)

    bias_in.wait()

    def interior(i, carry):
        for u in range(8):
            window(pl.multiple_of((8 * i + 2 + u) * QWIN, QWIN), False)
        return carry

    lax.fori_loop(0, 4, interior, 0)

    if comm:
        for side in range(2):
            halo_copy(side).wait_recv()
    project(0, RIM, False)
    project(ROWS + RIM, RIM, False)
    for w in (34, 35, 36, 37):
        window(w * QWIN, False)
    for w in (38, 39, 0, 1):
        window(w * QWIN, True)

    for part in range(5):
        span = pl.ds(part * 256, 256)
        values = ap[pl.ds(RIM + part * 256, 256), :].astype(F32)
        up[span, :] = (values + mm(mx[span, :], atom_out_ref[...])).astype(BF16)
    atoms_out = local(5, up, atom_update_hbm)

    tokens = iota((3 * TOK, WIDTH), 0) + (me - 1) * TOK
    for b in range(ROWS // WIDTH):
        named = slot_ref[b : b + 1, :]
        oh[:, b * WIDTH : (b + 1) * WIDTH] = (tokens == named).astype(F32).astype(BF16)

    def x_copy(side, c):
        device = (tok, left) if side == 0 else (tok, right)
        return send(
            sb.at[side, c], rb.at[side, c], x_send.at[side, c], x_recv.at[side, c], device
        )

    for c in range(CHUNKS):
        columns = slice(c * CHUNK, (c + 1) * CHUNK)
        for part in range(5):
            span = pl.ds(part * 256, 256)
            lf[span, :] = jnp.maximum(mm(up[span, :], agg_ref[:, columns]), 0.0).astype(BF16)
        lifted = lf[...]
        sb[0, c] = mm(oh[0:TOK, :], lifted).astype(BF16)
        sb[1, c] = mm(oh[2 * TOK : 3 * TOK, :], lifted).astype(BF16)
        if comm:
            go(x_copy(0, c))
            go(x_copy(1, c))
        own_sum[:, columns] = mm(oh[TOK : 2 * TOK, :], lifted)

    pair_in.wait()
    pair_weights = pair_weight_ref[...]

    def pair_bias(i, carry):
        for u in range(4):
            j = i * 8 + u * 2
            features = jnp.concatenate(
                [pair[j], pair[j + TOK // 2], pair[j + 1], pair[j + 1 + TOK // 2]], axis=0
            )
            both = mm_nt(pair_weights, features)
            start = pl.multiple_of(j * HEADS, 2 * HEADS)
            raw[pl.ds(start, HEADS), :] = both[:, :WIDTH]
            raw[pl.ds(start + HEADS, HEADS), :] = both[:, WIDTH:]
        return carry

    lax.fori_loop(0, 8, pair_bias, 0)
    half = TOK // 2
    first = iota((half, WIDTH), 1) < KEYS
    for g in range(HEADS // 2):
        even = raw[pl.ds(2 * g, half, stride=HEADS), :]
        odd = raw[pl.ds(2 * g + 1, half, stride=HEADS), :]
        columns = slice(g * WIDTH, (g + 1) * WIDTH)
        tb[0:half, columns] = jnp.where(first, even, pltpu.roll(odd, KEYS, 1)).astype(BF16)
        tb[half:TOK, columns] = jnp.where(first, pltpu.roll(even, KEYS, 1), odd).astype(BF16)

    for r in range(1, 8):
        forward(k_copy, r)
        forward(w_copy, r)
    for r in range(1, 8):
        forward(o_copy, r)

    for r in range(8):
        arrive(k_copy, r)
    half_ch = CH // 2
    span8 = 8 * KEYS
    member = lax.div(iota((span8, half_ch), 0), KEYS) == lax.div(iota((span8, half_ch), 1), HEAD)
    mbd[...] = member.astype(F32).astype(BF16)
    gathered = kv[...]
    keys = gathered[:, 0:4, :].reshape(KEYS, CH).astype(BF16)
    values = gathered[:, 4:8, :].reshape(KEYS, CH).astype(BF16)
    for g in range(2):
        columns = slice(g * half_ch, (g + 1) * half_ch)
        for h in range(8):
            span = slice(h * KEYS, (h + 1) * KEYS)
            kbd[g, span, :] = keys[:, columns] * mbd[span, :]
            vbd[g, span, :] = values[:, columns] * mbd[span, :]

    single_in.wait()
    if comm:
        for c in range(CHUNKS):
            for side in range(2):
                x_copy(side, c).wait_recv()
    counts = jnp.broadcast_to(count_ref[...].astype(F32), (TOK, TOK)).T
    inverse = 1.0 / counts
    for c in range(CHUNKS):
        columns = slice(c * CHUNK, (c + 1) * CHUNK)
        sums = own_sum[:, columns] + rb[0, c].astype(F32) + rb[1, c].astype(F32)
        per = jnp.concatenate([inverse, inverse], axis=1)
        acts[:, columns] = sums * per + single[:, columns].astype(F32)
    normed = layer_norm(acts[...], token_gain_ref[...]).astype(BF16)

    for r in range(8):
        arrive(w_copy, r)
    queries = mm_nt(normed, wq[0]).astype(BF16)
    gates = jax.nn.sigmoid(mm_nt(normed, wq[1]))

    token_scale = HEAD ** (-0.5)
    low = iota((TOK, WIDTH), 1) < KEYS
    gated = []
    for g in range(2):
        columns = slice(g * half_ch, (g + 1) * half_ch)
        scores = mm_nt(queries[:, columns], kbd[g]) * token_scale
        scores += tb[:, g * span8 : (g + 1) * span8].astype(F32)
        weights = []
        for i in range(4):
            part = scores[:, i * WIDTH : (i + 1) * WIDTH]
            top_low = jnp.max(jnp.where(low, part, -jnp.inf), axis=1, keepdims=True)
            top_high = jnp.max(jnp.where(low, -jnp.inf, part), axis=1, keepdims=True)
            weights.append(jnp.exp(part - jnp.where(low, top_low, top_high)).astype(BF16))
        weights = jnp.concatenate(weights, axis=1)
        mixed = mm(weights, vbd[g]) / mm(weights, mbd[...])
        gated.append((gates[:, columns] * mixed).astype(BF16))
    gated = jnp.concatenate(gated, axis=1)

    for r in range(8):
        arrive(o_copy, r)
    tu[...] = (acts[...] + mm(gated, wo[...])).astype(BF16)
    tokens_out = local(6, tu, token_update_hbm)
    for copy in sends:
        copy.wait_send()
    atoms_out.wait()
    tokens_out.wait()


def call(comm, *args):
    hbm = pl.BlockSpec(memory_space=pl.ANY)
    vmem = pl.BlockSpec(memory_space=pltpu.VMEM)
    v = pltpu.VMEM
    dma = pltpu.SemaphoreType.DMA
    return pl.pallas_call(
        functools.partial(kernel, comm),
        out_shape=(
            jax.ShapeDtypeStruct((ROWS, WIDTH), BF16),
            jax.ShapeDtypeStruct((TOK, CH), BF16),
        ),
        in_specs=[hbm, hbm, vmem, vmem, hbm, vmem, hbm] + [vmem] * 5 + [hbm, vmem, hbm],
        out_specs=(hbm, hbm),
        scratch_shapes=[
            v((PADDED, WIDTH), BF16),
            v((ROWS * ATOM_HEADS, KWIN), BF16),
            v((TOK, CH), BF16),
            v((TOK, KEYS, WIDTH), BF16),
            v((ROWS, WIDTH), BF16),
            v((PADDED, WIDTH), BF16),
            v((PADDED, 2 * WIDTH), BF16),
            v((ROWS, WIDTH), BF16),
            v((ROWS, WIDTH), BF16),
            v((3 * TOK, ROWS), BF16),
            v((ROWS, CHUNK), BF16),
            v((TOK, CH), F32),
            v((2, CHUNKS, TOK, CHUNK), BF16),
            v((2, CHUNKS, TOK, CHUNK), BF16),
            v((2, CH, CH), BF16),
            v((CH, CH), BF16),
            v((HEADS, 8, CH), F32),
            v((TOK // 2 * HEADS, WIDTH), F32),
            v((TOK, HEADS * KEYS), BF16),
            v((2, 8 * KEYS, CH // 2), BF16),
            v((2, 8 * KEYS, CH // 2), BF16),
            v((8 * KEYS, CH // 2), BF16),
            v((TOK, CH), F32),
            v((TOK, CH), BF16),
            dma((8,)),
            dma((2,)),
            dma((2,)),
            dma((16,)),
            dma((16,)),
            dma((16,)),
            dma((16,)),
            dma((16,)),
            dma((16,)),
            dma((2, CHUNKS)),
            dma((2, CHUNKS)),
        ],
        compiler_params=pltpu.CompilerParams(
            collective_id=0 if comm else None,
            has_side_effects=True,
            vmem_limit_bytes=60 * 1024 * 1024,
        ),
    )(*args)


def body(
    atoms,
    atom_bias,
    atom_token,
    token_atoms,
    token_single,
    key_value,
    pair,
    atom_gain,
    atom_qkv,
    atom_out_weight,
    agg_weight,
    token_gain,
    query_gate_weight,
    pair_weight,
    out_weight,
    comm=True,
):
    return call(
        comm,
        atoms,
        atom_bias.reshape(ROWS * ATOM_HEADS, KWIN),
        atom_token.reshape(ROWS // WIDTH, WIDTH),
        token_atoms.reshape(1, TOK),
        token_single,
        key_value,
        pair,
        atom_gain.reshape(1, WIDTH),
        atom_qkv,
        atom_out_weight,
        agg_weight,
        token_gain.reshape(1, CH),
        query_gate_weight.transpose(0, 2, 1),
        pair_weight.T,
        out_weight,
    )


def solution(mesh):
    return jax.shard_map(
        body,
        mesh=mesh,
        in_specs=(
            P(("tok", "atom"), None),
            P(("tok", "atom"), None, None),
            P(("tok", "atom")),
            P(("tok", "atom")),
            P(("tok", "atom"), None),
            P(None, "tok", None),
            P(("tok", "atom"), None, None),
            P(),
            P(),
            P(),
            P(),
            P(),
            P(None, None, "tok"),
            P(),
            P("tok", None),
        ),
        out_specs=(P(("tok", "atom"), None), P(("tok", "atom"), None)),
        check_vma=False,
    )
```

time: 154 us -> 47.1 us (0.31)
  the two profiles are of different devices: /device:TPU:1 before, /device:TPU:2 now
where the time goes in v1:
time: 47.1 us; the launch traced here: 46.8 us
  Pallas kernels  41.6 us (88%)
  local copies, waits for them, and re-layouts  4.6 us (10%)
  between operations  0.64 us (1%)
    pallas_call x1, Pallas kernels, call(): pl.pallas_call(functools.partial(kernel, comm), out_shape=(jax.ShapeDtype...  41.6 us
    unnamed x2, local copies, waits for them, and re-layouts  3.33 us
    reshape x1, local copies, waits for them, and re-layouts, body(): token_gain.reshape(1, CH)  1.27 us

profile of v1, /device:TPU:2, one launch (start us, length us, event | category | flops | bytes accessed | tf_op | source)
XLA Modules:
  0.0 46.8 jit_solution(1898034715355260346)
XLA Ops:
  0.6 1.3 %reshape.23.token_gain_ref = f32[1,768]{1,0:T(1,128)} reshape(f32[768]{0:T(1024)} %param.26) | data formatting | bytes 6144 | tf_op jit(solution)/shard_map/reshape | solution.py:487
  1.9 41.6 %shard_map.158 = (bf16[1280,128]{1,0:T(8,128)(2,1)}, bf16[128,768]{1,0:T(8,128)(2,1)}) custom-call(bf16[1280,128]{1,0:T(8,128)(2,1)} %atoms_hbm.1, bf16[5120,128]{1,0:T(8,128)(2,1)} %bitcast.6, s32[10,128]{1,0:T(8,128)} %bitcast.8, s32[1,128]{1,0:T(1,128)} %bitcast.10, bf16[128,768]{1,0:T(8,128)(2,1)} %single_hbm.1, bf16[2,4,768]{2,1,0:T(4,128)(2,1)} %kv_ref.1, ...), custom_call_target="tpu_custom_call" | custom-call | tf_op jit(solution)/shard_map/pallas_call | solution.py:403
  43.5 1.7 %copy.19 = bf16[1280,128]{1,0:T(8,128)(2,1)} copy(bf16[1280,128]{1,0:T(8,128)(2,1)} %get-tuple-element.4) | data formatting | bytes 655360
  45.2 1.6 %copy.20 = bf16[128,768]{1,0:T(8,128)(2,1)} copy(bf16[128,768]{1,0:T(8,128)(2,1)} %get-tuple-element.5) | data formatting | bytes 393216

commit v2 on v1

v2 whole, which is shorter than its diff:
```python
import functools

import jax
import jax.numpy as jnp
from jax import lax
from jax.experimental import pallas as pl
from jax.experimental.pallas import tpu as pltpu
from jax.sharding import PartitionSpec as P

MESH = pl.DeviceIdType.MESH
F32 = jnp.float32
BF16 = jnp.bfloat16

ATOM_HEADS = 4
QWIN = 32
KWIN = 128
RIM = 48
ROWS = 1280
PADDED = ROWS + 2 * RIM
WINDOWS = ROWS // QWIN
WIDTH = 128
TOK = 128
CH = 768
HEADS = 16
HEAD = 48
HALF = CH // 2
KEYS = 64
CHUNKS = 3
CHUNK = CH // CHUNKS
EPSILON = 1e-05
PIECES = ((0, 0), (0, 1), (0, -1), (1, 0), (0, 2), (1, 1), (1, -1), (1, 2))
NT = (((1,), (1,)), ((), ()))


def mm(a, b):
    return jnp.dot(a, b, preferred_element_type=F32)


def mm_nt(a, b):
    return lax.dot_general(a, b, NT, preferred_element_type=F32)


def iota(shape, axis):
    return lax.broadcasted_iota(jnp.int32, shape, axis)


def layer_norm(values, gain):
    centre = values - jnp.mean(values, axis=-1, keepdims=True)
    spread = jnp.mean(centre * centre, axis=-1, keepdims=True)
    return centre * lax.rsqrt(spread + EPSILON) * gain


def kernel(
    comm,
    atoms_hbm,
    bias_hbm,
    slot_hbm,
    count_hbm,
    single_hbm,
    kv_hbm,
    pair_hbm,
    atom_gain_hbm,
    qkv_hbm,
    atom_out_hbm,
    agg_hbm,
    token_gain_hbm,
    qg_hbm,
    pair_weight_hbm,
    out_hbm,
    up,
    tu,
    ap,
    bias,
    single,
    pair,
    qs,
    ks,
    kt,
    vs,
    mx,
    oh,
    lf,
    own_sum,
    sb,
    rb,
    wq,
    wo,
    kv,
    raw,
    tb,
    kbd,
    vbd,
    mbd,
    acts,
    slot_ref,
    count_ref,
    kv_ref,
    atom_gain_ref,
    qkv_ref,
    atom_out_ref,
    agg_ref,
    token_gain_ref,
    pair_weight_ref,
    local_sem,
    send_sem,
    halo_recv,
    w_recv,
    d_recv,
    o_recv,
    k_recv,
    wt_recv,
    ot_recv,
    kt_recv,
    x_recv,
):
    if comm:
        tok = lax.axis_index("tok")
        me = lax.axis_index("atom")
    else:
        tok = jnp.int32(5)
        me = jnp.int32(7)
    core = lax.rem(tok, 2)
    row = lax.rem(lax.div(tok, 2), 4)
    hi = lax.div(tok, 8)
    lo = lax.rem(me, 2)
    left = lax.rem(me + 31, 32)
    right = lax.rem(me + 1, 32)
    twin = tok + 1 - 2 * core

    def place(flip, step, who):
        high = 1 - hi if flip else hi
        return (high * 4 + lax.rem(row + step + 4, 4)) * 2 + who

    def origin(piece, who):
        flip, step = PIECES[piece]
        return place(flip, step, who)

    across = me + 1 - 2 * lo
    up_device = (place(0, 1, core), me)
    down_device = (place(0, -1, core), me)
    across_device = (place(1, 0, core), across)
    twin_device = (twin, me)
    left_device = (tok, left)
    right_device = (tok, right)
    targets = [(place(flip, -step, core), across if flip else me) for flip, step in PIECES]
    peers = targets[1:] + [twin_device, left_device, right_device]
    if comm:
        barrier = pltpu.get_barrier_semaphore()
        for peer in peers:
            pl.semaphore_signal(barrier, inc=1, device_id=peer, device_id_type=MESH)

    def local(i, src, dst):
        copy = pltpu.make_async_copy(src, dst, local_sem.at[i])
        copy.start()
        return copy

    def block(which):
        return pl.ds(pl.multiple_of(which * HEAD, 16), HEAD)

    qg_in = local(7, qg_hbm, wq.at[:, block(tok), :])
    out_in = local(1, out_hbm, wo.at[block(tok)])
    kv_in = local(8, kv_hbm, kv_ref)
    atoms_in = local(0, atoms_hbm, ap.at[pl.ds(RIM, ROWS)])
    gain_in = local(9, atom_gain_hbm, atom_gain_ref)
    qkv_in = local(10, qkv_hbm, qkv_ref)
    bias_in = local(2, bias_hbm, bias)
    small_in = [
        local(11, atom_out_hbm, atom_out_ref),
        local(12, agg_hbm, agg_ref),
        local(13, slot_hbm, slot_ref),
        local(14, count_hbm, count_ref),
        local(15, token_gain_hbm, token_gain_ref),
        local(16, pair_weight_hbm, pair_weight_ref),
    ]
    pair_in = local(3, pair_hbm, pair)
    single_in = local(4, single_hbm, single)

    started = []

    def send(src, dst, recv, device):
        return pltpu.make_async_remote_copy(
            src_ref=src, dst_ref=dst, send_sem=send_sem.at[len(started)], recv_sem=recv,
            device_id=device, device_id_type=MESH,
        )

    def go(ref, recv, device, target=None):
        if comm:
            copy = send(ref, ref if target is None else target, recv, device)
            copy.start()
            started.append(copy)

    def await_copy(ref, recv):
        if comm:
            send(ref, ref, recv, twin_device).wait_recv()

    def w_ref(piece, who):
        return wq.at[:, block(origin(piece, who)), :]

    def half_ref(piece, m):
        return wq.at[m, block(origin(piece, core)), :]

    def o_ref(piece, who):
        return wo.at[block(origin(piece, who))]

    def k_ref(piece, who):
        return kv.at[origin(piece, who)]

    def to_twin(ref_of, twin_recv, piece):
        go(ref_of(piece, core), twin_recv.at[piece], twin_device)

    def relay_first():
        for piece in (1, 2, 3):
            await_copy(w_ref(piece, core), w_recv.at[piece])
        go(half_ref(1, 0), d_recv.at[0], down_device)
        go(half_ref(2, 1), d_recv.at[1], up_device)
        go(w_ref(3, core), w_recv.at[6], up_device)
        go(w_ref(3, core), w_recv.at[5], down_device)
        for device, piece in ((up_device, 2), (down_device, 1), (across_device, 3)):
            go(o_ref(0, core), o_recv.at[piece], device)
        for piece in (1, 2, 3):
            to_twin(w_ref, wt_recv, piece)

    def relay_second():
        await_copy(half_ref(4, 0), d_recv.at[0])
        await_copy(half_ref(4, 1), d_recv.at[1])
        go(w_ref(4, core), w_recv.at[7], across_device)
        for piece in (1, 2, 3):
            await_copy(o_ref(piece, core), o_recv.at[piece])
        go(o_ref(1, core), o_recv.at[4], down_device)
        go(o_ref(3, core), o_recv.at[6], up_device)
        go(o_ref(3, core), o_recv.at[5], down_device)
        to_twin(w_ref, wt_recv, 4)
        for piece in (1, 2, 3):
            to_twin(o_ref, ot_recv, piece)
        for piece in range(1, 8):
            await_copy(k_ref(piece, core), k_recv.at[piece])
            to_twin(k_ref, kt_recv, piece)

    def relay_third():
        await_copy(o_ref(4, core), o_recv.at[4])
        go(o_ref(4, core), o_recv.at[7], across_device)
        for piece in (5, 6, 7):
            await_copy(w_ref(piece, core), w_recv.at[piece])
            to_twin(w_ref, wt_recv, piece)
        to_twin(o_ref, ot_recv, 4)

    def relay_fourth():
        for piece in (5, 6, 7):
            await_copy(o_ref(piece, core), o_recv.at[piece])
            to_twin(o_ref, ot_recv, piece)

    def arrive(ref_of, twin_recv):
        for piece in range(8):
            await_copy(ref_of(piece, 1 - core), twin_recv.at[piece])

    kv_in.wait()
    both = kv_ref[...].astype(F32)
    kv[tok] = jnp.concatenate(
        [both[0, :, :HALF], both[1, :, :HALF], both[0, :, HALF:], both[1, :, HALF:]], axis=0
    ).astype(BF16)
    qg_in.wait()
    atoms_in.wait()
    out_in.wait()
    if comm:
        pl.semaphore_wait(barrier, len(peers))
    for device, piece in ((up_device, 2), (down_device, 1), (across_device, 3)):
        go(w_ref(0, core), w_recv.at[piece], device)
    last, first = pl.ds(ROWS, RIM), pl.ds(RIM, RIM)
    low, high = pl.ds(0, RIM), pl.ds(ROWS + RIM, RIM)
    go(ap.at[last], halo_recv.at[0], right_device, ap.at[low])
    go(ap.at[first], halo_recv.at[1], left_device, ap.at[high])
    for piece in range(1, 8):
        go(k_ref(0, core), k_recv.at[piece], targets[piece])
    to_twin(w_ref, wt_recv, 0)
    to_twin(o_ref, ot_recv, 0)
    to_twin(k_ref, kt_recv, 0)

    def project(start, count, with_queries):
        values = ap[pl.ds(start, count), :].astype(F32)
        normed = layer_norm(values, atom_gain_ref[...]).astype(BF16)
        projected = mm(normed, qkv_ref[...]).astype(BF16)
        if with_queries:
            qs[pl.ds(start - RIM, count), :] = projected[:, :WIDTH]
        ks[pl.ds(start, count), :] = projected[:, WIDTH : 2 * WIDTH]
        vs[pl.ds(start, count), 0:WIDTH] = projected[:, 2 * WIDTH :]
        vs[pl.ds(start, count), WIDTH : 2 * WIDTH] = jnp.ones((count, WIDTH), BF16)

    gain_in.wait()
    qkv_in.wait()
    for part in range(5):
        project(RIM + part * 256, 256, True)

    lane = iota((QWIN, WIDTH), 1)
    head_of_lane = lax.div(lane, 32)
    head_masks = [(head_of_lane == h).astype(F32).astype(BF16) for h in range(ATOM_HEADS)]
    mix_row = iota((KWIN, KWIN), 0)
    mix_col = iota((KWIN, KWIN), 1)
    source = lax.rem(mix_row, QWIN) * ATOM_HEADS + lax.div(mix_row, QWIN)
    reorder = (mix_col == source).astype(F32).astype(BF16)
    scale = 32 ** (-0.5)
    low_end = jnp.where(me == 0, RIM, 0)
    high_end = jnp.where(me == 31, ROWS + RIM, PADDED)

    def window(w, edge):
        start = pl.multiple_of(w * QWIN, QWIN)
        queries = qs[pl.ds(start, QWIN), :]
        expanded = jnp.concatenate([queries * mask for mask in head_masks], axis=0)
        scores = mm(expanded, kt[w]) * scale
        scores += mm(reorder, bias[pl.ds(start * ATOM_HEADS, KWIN), :])
        if edge:
            place_of_key = start + mix_col
            inside = (place_of_key >= low_end) & (place_of_key < high_end)
            scores = jnp.where(inside, scores, -1e30)
        largest = jnp.max(scores, axis=1, keepdims=True)
        weights = jnp.exp(scores - largest).astype(BF16)
        both = mm(weights, vs[pl.ds(start, KWIN), :])
        rows = [both[h * QWIN : (h + 1) * QWIN] for h in range(ATOM_HEADS)]
        mixed, totals = rows[0][:, :WIDTH], rows[0][:, WIDTH:]
        for h in range(1, ATOM_HEADS):
            mixed = jnp.where(head_of_lane == h, rows[h][:, :WIDTH], mixed)
            totals = jnp.where(head_of_lane == h, rows[h][:, WIDTH:], totals)
        mx[pl.ds(start, QWIN), :] = (mixed / totals).astype(BF16)

    def transposed_keys(w):
        kt[w] = ks[pl.ds(pl.multiple_of(w * QWIN, QWIN), KWIN), :].T

    def turn(i, carry):
        for u in range(6):
            transposed_keys(6 * i + 2 + u)
        return carry

    lax.fori_loop(0, 6, turn, 0)
    bias_in.wait()

    def interior(i, carry):
        for u in range(8):
            window(8 * i + 2 + u, False)
        return carry

    lax.fori_loop(0, 4, interior, 0)

    relay_first()
    await_copy(ap.at[low], halo_recv.at[0])
    await_copy(ap.at[high], halo_recv.at[1])
    project(0, RIM, False)
    project(ROWS + RIM, RIM, False)
    for w in (38, 39, 0, 1):
        transposed_keys(w)
    for w in (34, 35, 36, 37):
        window(w, False)
    for w in (38, 39, 0, 1):
        window(w, True)

    for copy in small_in:
        copy.wait()
    for part in range(5):
        span = pl.ds(part * 256, 256)
        values = ap[pl.ds(RIM + part * 256, 256), :].astype(F32)
        up[span, :] = (values + mm(mx[span, :], atom_out_ref[...])).astype(BF16)

    tokens = iota((3 * TOK, WIDTH), 0) + (me - 1) * TOK
    for b in range(ROWS // WIDTH):
        named = slot_ref[b : b + 1, :]
        oh[:, b * WIDTH : (b + 1) * WIDTH] = (tokens == named).astype(F32).astype(BF16)

    for c in range(CHUNKS):
        columns = slice(c * CHUNK, (c + 1) * CHUNK)
        for part in range(5):
            span = pl.ds(part * 256, 256)
            lf[span, :] = jnp.maximum(mm(up[span, :], agg_ref[:, columns]), 0.0).astype(BF16)
        lifted = lf[...]
        sb[0, c] = mm(oh[0:TOK, :], lifted).astype(BF16)
        sb[1, c] = mm(oh[2 * TOK : 3 * TOK, :], lifted).astype(BF16)
        go(sb.at[0, c], x_recv.at[0, c], left_device, rb.at[0, c])
        go(sb.at[1, c], x_recv.at[1, c], right_device, rb.at[1, c])
        own_sum[:, columns] = mm(oh[TOK : 2 * TOK, :], lifted)

    relay_second()
    pair_in.wait()
    pair_weights = pair_weight_ref[...]

    def pair_bias(i, carry):
        for u in range(4):
            j = i * 8 + u * 2
            features = jnp.concatenate(
                [pair[j], pair[j + TOK // 2], pair[j + 1], pair[j + 1 + TOK // 2]], axis=0
            )
            both = mm_nt(pair_weights, features)
            start = pl.multiple_of(j * HEADS, 2 * HEADS)
            raw[pl.ds(start, HEADS), :] = both[:, :WIDTH]
            raw[pl.ds(start + HEADS, HEADS), :] = both[:, WIDTH:]
        return carry

    lax.fori_loop(0, 8, pair_bias, 0)
    relay_third()
    half = TOK // 2
    first_key = iota((half, WIDTH), 1) < KEYS
    for g in range(HEADS // 2):
        even = raw[pl.ds(2 * g, half, stride=HEADS), :]
        odd = raw[pl.ds(2 * g + 1, half, stride=HEADS), :]
        columns = slice(g * WIDTH, (g + 1) * WIDTH)
        tb[0:half, columns] = jnp.where(first_key, even, pltpu.roll(odd, KEYS, 1)).astype(BF16)
        tb[half:TOK, columns] = jnp.where(first_key, pltpu.roll(even, KEYS, 1), odd).astype(BF16)

    arrive(k_ref, kt_recv)
    span8 = 8 * KEYS
    member = lax.div(iota((span8, HALF), 0), KEYS) == lax.div(iota((span8, HALF), 1), HEAD)
    mbd[...] = member.astype(F32).astype(BF16)
    gathered = kv[...].astype(F32)
    for g in range(2):
        keys = gathered[:, 8 * g : 8 * g + 4, :].reshape(KEYS, HALF).astype(BF16)
        values = gathered[:, 8 * g + 4 : 8 * g + 8, :].reshape(KEYS, HALF).astype(BF16)
        for h in range(8):
            span = slice(h * KEYS, (h + 1) * KEYS)
            kbd[g, span, :] = keys * mbd[span, :]
            vbd[g, span, :] = values * mbd[span, :]

    relay_fourth()
    single_in.wait()
    for c in range(CHUNKS):
        for side in range(2):
            await_copy(rb.at[side, c], x_recv.at[side, c])
    counts = jnp.broadcast_to(count_ref[...].astype(F32), (TOK, TOK)).T
    inverse = 1.0 / counts
    for c in range(CHUNKS):
        columns = slice(c * CHUNK, (c + 1) * CHUNK)
        sums = own_sum[:, columns] + rb[0, c].astype(F32) + rb[1, c].astype(F32)
        per = jnp.concatenate([inverse, inverse], axis=1)
        acts[:, columns] = sums * per + single[:, columns].astype(F32)
    gain = jnp.concatenate([token_gain_ref[i : i + 1, :] for i in range(CH // WIDTH)], axis=1)
    normed = layer_norm(acts[...], gain).astype(BF16)

    arrive(w_ref, wt_recv)
    queries = mm_nt(normed, wq[0]).astype(BF16)
    gates = jax.nn.sigmoid(mm_nt(normed, wq[1]))

    token_scale = HEAD ** (-0.5)
    low = iota((TOK, WIDTH), 1) < KEYS
    gated = []
    for g in range(2):
        columns = slice(g * HALF, (g + 1) * HALF)
        scores = mm_nt(queries[:, columns], kbd[g]) * token_scale
        scores += tb[:, g * span8 : (g + 1) * span8].astype(F32)
        weights = []
        for i in range(4):
            part = scores[:, i * WIDTH : (i + 1) * WIDTH]
            top_low = jnp.max(jnp.where(low, part, -jnp.inf), axis=1, keepdims=True)
            top_high = jnp.max(jnp.where(low, -jnp.inf, part), axis=1, keepdims=True)
            weights.append(jnp.exp(part - jnp.where(low, top_low, top_high)).astype(BF16))
        weights = jnp.concatenate(weights, axis=1)
        mixed = mm(weights, vbd[g]) / mm(weights, mbd[...])
        gated.append((gates[:, columns] * mixed).astype(BF16))
    gated = jnp.concatenate(gated, axis=1)

    arrive(o_ref, ot_recv)
    tu[...] = (acts[...] + mm(gated, wo[...])).astype(BF16)
    for copy in started:
        copy.wait_send()


def call(comm, *args):
    hbm = pl.BlockSpec(memory_space=pl.ANY)
    v = pltpu.VMEM
    dma = pltpu.SemaphoreType.DMA
    return pl.pallas_call(
        functools.partial(kernel, comm),
        out_shape=(v((ROWS, WIDTH), BF16), v((TOK, CH), BF16)),
        in_specs=[hbm] * 15,
        out_specs=(pl.BlockSpec(memory_space=v), pl.BlockSpec(memory_space=v)),
        scratch_shapes=[
            v((PADDED, WIDTH), BF16),
            v((ROWS * ATOM_HEADS, KWIN), BF16),
            v((TOK, CH), BF16),
            v((TOK, KEYS, WIDTH), BF16),
            v((ROWS, WIDTH), BF16),
            v((PADDED, WIDTH), BF16),
            v((WINDOWS, WIDTH, KWIN), BF16),
            v((PADDED, 2 * WIDTH), BF16),
            v((ROWS, WIDTH), BF16),
            v((3 * TOK, ROWS), BF16),
            v((ROWS, CHUNK), BF16),
            v((TOK, CH), F32),
            v((2, CHUNKS, TOK, CHUNK), BF16),
            v((2, CHUNKS, TOK, CHUNK), BF16),
            v((2, CH, CH), BF16),
            v((CH, CH), BF16),
            v((HEADS, 16, CH // 2), BF16),
            v((TOK // 2 * HEADS, WIDTH), F32),
            v((TOK, HEADS * KEYS), BF16),
            v((2, 8 * KEYS, CH // 2), BF16),
            v((2, 8 * KEYS, CH // 2), BF16),
            v((8 * KEYS, CH // 2), BF16),
            v((TOK, CH), F32),
            v((ROWS // WIDTH, WIDTH), jnp.int32),
            v((1, TOK), jnp.int32),
            v((2, 4, CH), BF16),
            v((1, WIDTH), F32),
            v((WIDTH, 3 * WIDTH), BF16),
            v((WIDTH, WIDTH), BF16),
            v((WIDTH, CH), BF16),
            v((CH // WIDTH, WIDTH), F32),
            v((HEADS, WIDTH), BF16),
            dma((17,)),
            dma((72,)),
            dma((2,)),
            dma((8,)),
            dma((2,)),
            dma((8,)),
            dma((8,)),
            dma((8,)),
            dma((8,)),
            dma((8,)),
            dma((2, CHUNKS)),
        ],
        compiler_params=pltpu.CompilerParams(
            collective_id=0 if comm else None,
            has_side_effects=True,
            vmem_limit_bytes=60 * 1024 * 1024,
        ),
    )(*args)


def write_kernel(up, tu, atom_update, token_update, sems):
    copies = [
        pltpu.make_async_copy(up, atom_update, sems.at[0]),
        pltpu.make_async_copy(tu, token_update, sems.at[1]),
    ]
    for copy in copies:
        copy.start()
    for copy in copies:
        copy.wait()


def write(up, tu):
    hbm = pl.BlockSpec(memory_space=pl.ANY)
    return pl.pallas_call(
        write_kernel,
        out_shape=(
            jax.ShapeDtypeStruct((ROWS, WIDTH), BF16),
            jax.ShapeDtypeStruct((TOK, CH), BF16),
        ),
        in_specs=[pl.BlockSpec(memory_space=pltpu.VMEM)] * 2,
        out_specs=(hbm, hbm),
        scratch_shapes=[pltpu.SemaphoreType.DMA((2,))],
        compiler_params=pltpu.CompilerParams(vmem_limit_bytes=8 * 1024 * 1024),
    )(up, tu)


def body(
    atoms,
    atom_bias,
    atom_token,
    token_atoms,
    token_single,
    key_value,
    pair,
    atom_gain,
    atom_qkv,
    atom_out_weight,
    agg_weight,
    token_gain,
    query_gate_weight,
    pair_weight,
    out_weight,
    comm=True,
):
    up, tu = call(
        comm,
        atoms,
        atom_bias.reshape(ROWS * ATOM_HEADS, KWIN),
        atom_token.reshape(ROWS // WIDTH, WIDTH),
        token_atoms.reshape(1, TOK),
        token_single,
        key_value,
        pair,
        atom_gain.reshape(1, WIDTH),
        atom_qkv,
        atom_out_weight,
        agg_weight,
        token_gain.reshape(CH // WIDTH, WIDTH),
        query_gate_weight.transpose(0, 2, 1),
        pair_weight.T,
        out_weight,
    )
    return write(up, tu)


def solution(mesh):
    return jax.shard_map(
        body,
        mesh=mesh,
        in_specs=(
            P(("tok", "atom"), None),
            P(("tok", "atom"), None, None),
            P(("tok", "atom")),
            P(("tok", "atom")),
            P(("tok", "atom"), None),
            P(None, "tok", None),
            P(("tok", "atom"), None, None),
            P(),
            P(),
            P(),
            P(),
            P(),
            P(None, None, "tok"),
            P(),
            P("tok", None),
        ),
        out_specs=(P(("tok", "atom"), None), P(("tok", "atom"), None)),
        check_vma=False,
    )
```

time: 47.1 us -> 38.2 us (0.81)
  the two profiles are of different devices: /device:TPU:2 before, /device:TPU:1 now
where the time goes in v2:
time: 38.2 us; the launch traced here: 37.8 us
  Pallas kernels  37.2 us (97%)
  between operations  0.64 us (2%)
    pallas_call x1, Pallas kernels, call(): pl.pallas_call(functools.partial(kernel, comm), out_shape=(v((ROWS, WIDTH...  36.4 us
    pallas_call x1, Pallas kernels, write(): pl.pallas_call(write_kernel, out_shape=(jax.ShapeDtypeStruct((ROWS, WIDTH...  0.8 us

profile of v2, /device:TPU:1, one launch (start us, length us, event | category | flops | bytes accessed | tf_op | source)
XLA Modules:
  0.0 37.8 jit_solution(10010490889713178749)
XLA Ops:
  0.6 36.4 %shard_map.158 = (bf16[1280,128]{1,0:T(8,128)(2,1)S(1)}, bf16[128,768]{1,0:T(8,128)(2,1)S(1)}) custom-call(bf16[1280,128]{1,0:T(8,128)(2,1)} %atoms_hbm.1, bf16[5120,128]{1,0:T(8,128)(2,1)} %bitcast.7, s32[10,128]{1,0:T(8,128)} %bitcast.9, s32[1,128]{1,0:T(1,128)} %bitcast.12, bf16[128,768]{1,0:T(8,128)(2,1)} %single_hbm.1, bf16[2,4,768]{2,1,0:T(4,128)(2,1)} %kv_hbm.1, ...), custom_call_target="tpu_custom_call" | custom-call | tf_op jit(solution)/shard_map/pallas_call | solution.py:465
  37.0 0.8 %shard_map.159 = (bf16[1280,128]{1,0:T(8,128)(2,1)}, bf16[128,768]{1,0:T(8,128)(2,1)}) custom-call(bf16[1280,128]{1,0:T(8,128)(2,1)S(1)} %get-tuple-element.4.up, bf16[128,768]{1,0:T(8,128)(2,1)S(1)} %get-tuple-element.5.tu), custom_call_target="tpu_custom_call" | custom-call | tf_op jit(solution)/shard_map/pallas_call | solution.py:536

commit v3 on v2

--- a/solution.py
+++ b/solution.py
@@ -29,6 +29,7 @@
 CHUNK = CH // CHUNKS
 EPSILON = 1e-05
 PIECES = ((0, 0), (0, 1), (0, -1), (1, 0), (0, 2), (1, 1), (1, -1), (1, 2))
+OWN, AHEAD, BEHIND, ACROSS, FAR, NEAR_ACROSS, OTHER_ACROSS, FAR_ACROSS = range(8)
 NT = (((1,), (1,)), ((), ()))
 
 
@@ -104,12 +105,9 @@
     local_sem,
     send_sem,
     halo_recv,
-    w_recv,
-    d_recv,
-    o_recv,
+    u_recv,
+    twin_recv,
     k_recv,
-    wt_recv,
-    ot_recv,
     kt_recv,
     x_recv,
 ):
@@ -131,9 +129,11 @@
         high = 1 - hi if flip else hi
         return (high * 4 + lax.rem(row + step + 4, 4)) * 2 + who
 
+    sign = 1 - 2 * lax.rem(lax.div(me, 2), 2)
+
     def origin(piece, who):
         flip, step = PIECES[piece]
-        return place(flip, step, who)
+        return place(flip, step if piece < FAR else sign * step, who)
 
     across = me + 1 - 2 * lo
     up_device = (place(0, 1, core), me)
@@ -142,8 +142,15 @@
     twin_device = (twin, me)
     left_device = (tok, left)
     right_device = (tok, right)
-    targets = [(place(flip, -step, core), across if flip else me) for flip, step in PIECES]
-    peers = targets[1:] + [twin_device, left_device, right_device]
+    sign_device = (place(0, sign, core), me)
+    back_device = (place(0, -sign, core), me)
+    above_device = (tok, lax.rem(me + 2, 32))
+    below_device = (tok, lax.rem(me + 30, 32))
+    targets = []
+    for piece, (flip, step) in enumerate(PIECES):
+        steps = -step if piece < FAR else -sign * step
+        targets.append((place(flip, steps, core), across if flip else me))
+    peers = targets[1:] + [twin_device, left_device, right_device, above_device, below_device]
     if comm:
         barrier = pltpu.get_barrier_semaphore()
         for peer in peers:
@@ -163,11 +170,11 @@
     atoms_in = local(0, atoms_hbm, ap.at[pl.ds(RIM, ROWS)])
     gain_in = local(9, atom_gain_hbm, atom_gain_ref)
     qkv_in = local(10, qkv_hbm, qkv_ref)
+    slot_in = local(13, slot_hbm, slot_ref)
     bias_in = local(2, bias_hbm, bias)
     small_in = [
         local(11, atom_out_hbm, atom_out_ref),
         local(12, agg_hbm, agg_ref),
-        local(13, slot_hbm, slot_ref),
         local(14, count_hbm, count_ref),
         local(15, token_gain_hbm, token_gain_ref),
         local(16, pair_weight_hbm, pair_weight_ref),
@@ -193,65 +200,52 @@
         if comm:
             send(ref, ref, recv, twin_device).wait_recv()
 
-    def w_ref(piece, who):
-        return wq.at[:, block(origin(piece, who)), :]
-
-    def half_ref(piece, m):
-        return wq.at[m, block(origin(piece, core)), :]
-
-    def o_ref(piece, who):
-        return wo.at[block(origin(piece, who))]
+    def unit_ref(tok_of, unit):
+        return wq.at[unit, block(tok_of), :] if unit < 2 else wo.at[block(tok_of)]
 
     def k_ref(piece, who):
         return kv.at[origin(piece, who)]
 
-    def to_twin(ref_of, twin_recv, piece):
-        go(ref_of(piece, core), twin_recv.at[piece], twin_device)
-
-    def relay_first():
-        for piece in (1, 2, 3):
-            await_copy(w_ref(piece, core), w_recv.at[piece])
-        go(half_ref(1, 0), d_recv.at[0], down_device)
-        go(half_ref(2, 1), d_recv.at[1], up_device)
-        go(w_ref(3, core), w_recv.at[6], up_device)
-        go(w_ref(3, core), w_recv.at[5], down_device)
-        for device, piece in ((up_device, 2), (down_device, 1), (across_device, 3)):
-            go(o_ref(0, core), o_recv.at[piece], device)
-        for piece in (1, 2, 3):
-            to_twin(w_ref, wt_recv, piece)
-
-    def relay_second():
-        await_copy(half_ref(4, 0), d_recv.at[0])
-        await_copy(half_ref(4, 1), d_recv.at[1])
-        go(w_ref(4, core), w_recv.at[7], across_device)
-        for piece in (1, 2, 3):
-            await_copy(o_ref(piece, core), o_recv.at[piece])
-        go(o_ref(1, core), o_recv.at[4], down_device)
-        go(o_ref(3, core), o_recv.at[6], up_device)
-        go(o_ref(3, core), o_recv.at[5], down_device)
-        to_twin(w_ref, wt_recv, 4)
-        for piece in (1, 2, 3):
-            to_twin(o_ref, ot_recv, piece)
+    def pass_on(piece, unit, name, device):
+        go(unit_ref(origin(piece, core), unit), u_recv.at[name, unit], device)
+
+    def direct(unit):
+        pass_on(OWN, unit, BEHIND, up_device)
+        pass_on(OWN, unit, AHEAD, down_device)
+        pass_on(OWN, unit, ACROSS, across_device)
+
+    def take(unit, pieces):
+        for piece in pieces:
+            await_copy(unit_ref(origin(piece, core), unit), u_recv.at[piece, unit])
+
+    def to_twin(unit, pieces):
+        for piece in pieces:
+            go(unit_ref(origin(piece, core), unit), twin_recv.at[piece, unit], twin_device)
+
+    def relay_first(unit):
+        take(unit, (AHEAD, BEHIND, ACROSS))
+        go(unit_ref(place(0, -sign, core), unit), u_recv.at[FAR, unit], sign_device)
+        pass_on(ACROSS, unit, NEAR_ACROSS, back_device)
+        to_twin(unit, (AHEAD, BEHIND, ACROSS))
+
+    def relay_second(unit):
+        take(unit, (FAR, NEAR_ACROSS))
+        pass_on(FAR, unit, FAR_ACROSS, across_device)
+        pass_on(NEAR_ACROSS, unit, OTHER_ACROSS, below_device if unit == 1 else above_device)
+        to_twin(unit, (FAR, NEAR_ACROSS))
+
+    def relay_third(unit):
+        take(unit, (OTHER_ACROSS, FAR_ACROSS))
+        to_twin(unit, (OTHER_ACROSS, FAR_ACROSS))
+
+    def relay_keys():
         for piece in range(1, 8):
             await_copy(k_ref(piece, core), k_recv.at[piece])
-            to_twin(k_ref, kt_recv, piece)
-
-    def relay_third():
-        await_copy(o_ref(4, core), o_recv.at[4])
-        go(o_ref(4, core), o_recv.at[7], across_device)
-        for piece in (5, 6, 7):
-            await_copy(w_ref(piece, core), w_recv.at[piece])
-            to_twin(w_ref, wt_recv, piece)
-        to_twin(o_ref, ot_recv, 4)
-
-    def relay_fourth():
-        for piece in (5, 6, 7):
-            await_copy(o_ref(piece, core), o_recv.at[piece])
-            to_twin(o_ref, ot_recv, piece)
-
-    def arrive(ref_of, twin_recv):
+            go(k_ref(piece, core), kt_recv.at[piece], twin_device)
+
+    def arrive(unit):
         for piece in range(8):
-            await_copy(ref_of(piece, 1 - core), twin_recv.at[piece])
+            await_copy(unit_ref(origin(piece, 1 - core), unit), twin_recv.at[piece, unit])
 
     kv_in.wait()
     both = kv_ref[...].astype(F32)
@@ -261,19 +255,26 @@
     qg_in.wait()
     atoms_in.wait()
     out_in.wait()
+    slot_in.wait()
+    tokens = iota((3 * TOK, WIDTH), 0) + (me - 1) * TOK
+    for b in range(ROWS // WIDTH):
+        named = slot_ref[b : b + 1, :]
+        oh[:, b * WIDTH : (b + 1) * WIDTH] = (tokens == named).astype(F32).astype(BF16)
+    span8 = 8 * KEYS
+    member = lax.div(iota((span8, HALF), 0), KEYS) == lax.div(iota((span8, HALF), 1), HEAD)
+    mbd[...] = member.astype(F32).astype(BF16)
     if comm:
         pl.semaphore_wait(barrier, len(peers))
-    for device, piece in ((up_device, 2), (down_device, 1), (across_device, 3)):
-        go(w_ref(0, core), w_recv.at[piece], device)
+    direct(0)
     last, first = pl.ds(ROWS, RIM), pl.ds(RIM, RIM)
     low, high = pl.ds(0, RIM), pl.ds(ROWS + RIM, RIM)
     go(ap.at[last], halo_recv.at[0], right_device, ap.at[low])
     go(ap.at[first], halo_recv.at[1], left_device, ap.at[high])
     for piece in range(1, 8):
         go(k_ref(0, core), k_recv.at[piece], targets[piece])
-    to_twin(w_ref, wt_recv, 0)
-    to_twin(o_ref, ot_recv, 0)
-    to_twin(k_ref, kt_recv, 0)
+    go(k_ref(OWN, core), kt_recv.at[OWN], twin_device)
+    for unit in range(3):
+        to_twin(unit, (OWN,))
 
     def project(start, count, with_queries):
         values = ap[pl.ds(start, count), :].astype(F32)
@@ -290,6 +291,7 @@
     for part in range(5):
         project(RIM + part * 256, 256, True)
 
+    direct(1)
     lane = iota((QWIN, WIDTH), 1)
     head_of_lane = lax.div(lane, 32)
     head_masks = [(head_of_lane == h).astype(F32).astype(BF16) for h in range(ATOM_HEADS)]
@@ -330,6 +332,7 @@
         return carry
 
     lax.fori_loop(0, 6, turn, 0)
+    direct(2)
     bias_in.wait()
 
     def interior(i, carry):
@@ -337,9 +340,11 @@
             window(8 * i + 2 + u, False)
         return carry
 
-    lax.fori_loop(0, 4, interior, 0)
-
-    relay_first()
+    lax.fori_loop(0, 2, interior, 0)
+    relay_first(0)
+    lax.fori_loop(2, 4, interior, 0)
+
+    relay_first(1)
     await_copy(ap.at[low], halo_recv.at[0])
     await_copy(ap.at[high], halo_recv.at[1])
     project(0, RIM, False)
@@ -351,6 +356,7 @@
     for w in (38, 39, 0, 1):
         window(w, True)
 
+    relay_first(2)
     for copy in small_in:
         copy.wait()
     for part in range(5):
@@ -358,24 +364,21 @@
         values = ap[pl.ds(RIM + part * 256, 256), :].astype(F32)
         up[span, :] = (values + mm(mx[span, :], atom_out_ref[...])).astype(BF16)
 
-    tokens = iota((3 * TOK, WIDTH), 0) + (me - 1) * TOK
-    for b in range(ROWS // WIDTH):
-        named = slot_ref[b : b + 1, :]
-        oh[:, b * WIDTH : (b + 1) * WIDTH] = (tokens == named).astype(F32).astype(BF16)
-
+    relay_second(0)
     for c in range(CHUNKS):
         columns = slice(c * CHUNK, (c + 1) * CHUNK)
         for part in range(5):
             span = pl.ds(part * 256, 256)
-            lf[span, :] = jnp.maximum(mm(up[span, :], agg_ref[:, columns]), 0.0).astype(BF16)
-        lifted = lf[...]
+            lf[c, span, :] = jnp.maximum(mm(up[span, :], agg_ref[:, columns]), 0.0).astype(BF16)
+        lifted = lf[c]
         sb[0, c] = mm(oh[0:TOK, :], lifted).astype(BF16)
         sb[1, c] = mm(oh[2 * TOK : 3 * TOK, :], lifted).astype(BF16)
         go(sb.at[0, c], x_recv.at[0, c], left_device, rb.at[0, c])
         go(sb.at[1, c], x_recv.at[1, c], right_device, rb.at[1, c])
-        own_sum[:, columns] = mm(oh[TOK : 2 * TOK, :], lifted)
-
-    relay_second()
+    relay_second(1)
+    for c in range(CHUNKS):
+        own_sum[:, c * CHUNK : (c + 1) * CHUNK] = mm(oh[TOK : 2 * TOK, :], lf[c])
+
     pair_in.wait()
     pair_weights = pair_weight_ref[...]
 
@@ -391,8 +394,11 @@
             raw[pl.ds(start + HEADS, HEADS), :] = both[:, WIDTH:]
         return carry
 
-    lax.fori_loop(0, 8, pair_bias, 0)
-    relay_third()
+    lax.fori_loop(0, 4, pair_bias, 0)
+    relay_second(2)
+    lax.fori_loop(4, 8, pair_bias, 0)
+    relay_third(0)
+    relay_keys()
     half = TOK // 2
     first_key = iota((half, WIDTH), 1) < KEYS
     for g in range(HEADS // 2):
@@ -402,20 +408,19 @@
         tb[0:half, columns] = jnp.where(first_key, even, pltpu.roll(odd, KEYS, 1)).astype(BF16)
         tb[half:TOK, columns] = jnp.where(first_key, pltpu.roll(even, KEYS, 1), odd).astype(BF16)
 
-    arrive(k_ref, kt_recv)
-    span8 = 8 * KEYS
-    member = lax.div(iota((span8, HALF), 0), KEYS) == lax.div(iota((span8, HALF), 1), HEAD)
-    mbd[...] = member.astype(F32).astype(BF16)
+    relay_third(1)
+    for piece in range(8):
+        await_copy(k_ref(piece, 1 - core), kt_recv.at[piece])
     gathered = kv[...].astype(F32)
     for g in range(2):
         keys = gathered[:, 8 * g : 8 * g + 4, :].reshape(KEYS, HALF).astype(BF16)
         values = gathered[:, 8 * g + 4 : 8 * g + 8, :].reshape(KEYS, HALF).astype(BF16)
         for h in range(8):
             span = slice(h * KEYS, (h + 1) * KEYS)
-            kbd[g, span, :] = keys * mbd[span, :]
             vbd[g, span, :] = values * mbd[span, :]
-
-    relay_fourth()
+        kbd[g] = (jnp.concatenate([keys] * 8, axis=0) * mbd[...]).T
+
+    relay_third(2)
     single_in.wait()
     for c in range(CHUNKS):
         for side in range(2):
@@ -430,7 +435,8 @@
     gain = jnp.concatenate([token_gain_ref[i : i + 1, :] for i in range(CH // WIDTH)], axis=1)
     normed = layer_norm(acts[...], gain).astype(BF16)
 
-    arrive(w_ref, wt_recv)
+    arrive(0)
+    arrive(1)
     queries = mm_nt(normed, wq[0]).astype(BF16)
     gates = jax.nn.sigmoid(mm_nt(normed, wq[1]))
 
@@ -439,7 +445,7 @@
     gated = []
     for g in range(2):
         columns = slice(g * HALF, (g + 1) * HALF)
-        scores = mm_nt(queries[:, columns], kbd[g]) * token_scale
+        scores = mm(queries[:, columns], kbd[g]) * token_scale
         scores += tb[:, g * span8 : (g + 1) * span8].astype(F32)
         weights = []
         for i in range(4):
@@ -452,7 +458,7 @@
         gated.append((gates[:, columns] * mixed).astype(BF16))
     gated = jnp.concatenate(gated, axis=1)
 
-    arrive(o_ref, ot_recv)
+    arrive(2)
     tu[...] = (acts[...] + mm(gated, wo[...])).astype(BF16)
     for copy in started:
         copy.wait_send()
@@ -478,7 +484,7 @@
             v((PADDED, 2 * WIDTH), BF16),
             v((ROWS, WIDTH), BF16),
             v((3 * TOK, ROWS), BF16),
-            v((ROWS, CHUNK), BF16),
+            v((CHUNKS, ROWS, CHUNK), BF16),
             v((TOK, CH), F32),
             v((2, CHUNKS, TOK, CHUNK), BF16),
             v((2, CHUNKS, TOK, CHUNK), BF16),
@@ -487,8 +493,8 @@
             v((HEADS, 16, CH // 2), BF16),
             v((TOK // 2 * HEADS, WIDTH), F32),
             v((TOK, HEADS * KEYS), BF16),
-            v((2, 8 * KEYS, CH // 2), BF16),
-            v((2, 8 * KEYS, CH // 2), BF16),
+            v((2, HALF, 8 * KEYS), BF16),
+            v((2, 8 * KEYS, HALF), BF16),
             v((8 * KEYS, CH // 2), BF16),
             v((TOK, CH), F32),
             v((ROWS // WIDTH, WIDTH), jnp.int32),
@@ -501,13 +507,10 @@
             v((CH // WIDTH, WIDTH), F32),
             v((HEADS, WIDTH), BF16),
             dma((17,)),
-            dma((72,)),
+            dma((80,)),
             dma((2,)),
-            dma((8,)),
-            dma((2,)),
-            dma((8,)),
-            dma((8,)),
-            dma((8,)),
+            dma((8, 3,)),
+            dma((8, 3,)),
             dma((8,)),
             dma((8,)),
             dma((2, CHUNKS)),

time: 38.2 us -> 37.3 us (0.976)
  Pallas kernels: 37.2 us -> 36.5 us
    pallas_call x1, Pallas kernels: 36.4 us -> 35.7 us  [call(): pl.pallas_call(functools.partial(kernel, comm), out_shape=(v((ROWS, WIDTH...]
where the time goes in v3:
time: 37.3 us; the launch traced here: 37.2 us
  Pallas kernels  36.5 us (98%)
  between operations  0.64 us (2%)
    pallas_call x1, Pallas kernels, call(): pl.pallas_call(functools.partial(kernel, comm), out_shape=(v((ROWS, WIDTH...  35.7 us
    pallas_call x1, Pallas kernels, write(): pl.pallas_call(write_kernel, out_shape=(jax.ShapeDtypeStruct((ROWS, WIDTH...  0.8 us

profile of v3, /device:TPU:1, one launch (start us, length us, event | category | flops | bytes accessed | tf_op | source)
XLA Modules:
  0.0 37.2 jit_solution(1846212417193482161)
XLA Ops:
  0.6 35.7 %shard_map.158 = (bf16[1280,128]{1,0:T(8,128)(2,1)S(1)}, bf16[128,768]{1,0:T(8,128)(2,1)S(1)}) custom-call(bf16[1280,128]{1,0:T(8,128)(2,1)} %atoms_hbm.1, bf16[5120,128]{1,0:T(8,128)(2,1)} %bitcast.7, s32[10,128]{1,0:T(8,128)} %bitcast.9, s32[1,128]{1,0:T(1,128)} %bitcast.12, bf16[128,768]{1,0:T(8,128)(2,1)} %single_hbm.1, bf16[2,4,768]{2,1,0:T(4,128)(2,1)} %kv_hbm.1, ...), custom_call_target="tpu_custom_call" | custom-call | tf_op jit(solution)/shard_map/pallas_call | solution.py:471
  36.4 0.8 %shard_map.159 = (bf16[1280,128]{1,0:T(8,128)(2,1)}, bf16[128,768]{1,0:T(8,128)(2,1)}) custom-call(bf16[1280,128]{1,0:T(8,128)(2,1)S(1)} %get-tuple-element.4.up, bf16[128,768]{1,0:T(8,128)(2,1)S(1)} %get-tuple-element.5.tu), custom_call_target="tpu_custom_call" | custom-call | tf_op jit(solution)/shard_map/pallas_call | solution.py:539

commit v4 on v3

--- a/solution.py
+++ b/solution.py
@@ -107,8 +107,6 @@
     halo_recv,
     u_recv,
     twin_recv,
-    k_recv,
-    kt_recv,
     x_recv,
 ):
     if comm:
@@ -146,11 +144,7 @@
     back_device = (place(0, -sign, core), me)
     above_device = (tok, lax.rem(me + 2, 32))
     below_device = (tok, lax.rem(me + 30, 32))
-    targets = []
-    for piece, (flip, step) in enumerate(PIECES):
-        steps = -step if piece < FAR else -sign * step
-        targets.append((place(flip, steps, core), across if flip else me))
-    peers = targets[1:] + [twin_device, left_device, right_device, above_device, below_device]
+    peers = [up_device, down_device, across_device, twin_device, left_device, right_device, above_device, below_device]
     if comm:
         barrier = pltpu.get_barrier_semaphore()
         for peer in peers:
@@ -201,10 +195,9 @@
             send(ref, ref, recv, twin_device).wait_recv()
 
     def unit_ref(tok_of, unit):
+        if unit == 3:
+            return kv.at[tok_of]
         return wq.at[unit, block(tok_of), :] if unit < 2 else wo.at[block(tok_of)]
-
-    def k_ref(piece, who):
-        return kv.at[origin(piece, who)]
 
     def pass_on(piece, unit, name, device):
         go(unit_ref(origin(piece, core), unit), u_recv.at[name, unit], device)
@@ -237,11 +230,6 @@
     def relay_third(unit):
         take(unit, (OTHER_ACROSS, FAR_ACROSS))
         to_twin(unit, (OTHER_ACROSS, FAR_ACROSS))
-
-    def relay_keys():
-        for piece in range(1, 8):
-            await_copy(k_ref(piece, core), k_recv.at[piece])
-            go(k_ref(piece, core), kt_recv.at[piece], twin_device)
 
     def arrive(unit):
         for piece in range(8):
@@ -270,11 +258,6 @@
     low, high = pl.ds(0, RIM), pl.ds(ROWS + RIM, RIM)
     go(ap.at[last], halo_recv.at[0], right_device, ap.at[low])
     go(ap.at[first], halo_recv.at[1], left_device, ap.at[high])
-    for piece in range(1, 8):
-        go(k_ref(0, core), k_recv.at[piece], targets[piece])
-    go(k_ref(OWN, core), kt_recv.at[OWN], twin_device)
-    for unit in range(3):
-        to_twin(unit, (OWN,))
 
     def project(start, count, with_queries):
         values = ap[pl.ds(start, count), :].astype(F32)
@@ -332,6 +315,7 @@
         return carry
 
     lax.fori_loop(0, 6, turn, 0)
+    direct(3)
     direct(2)
     bias_in.wait()
 
@@ -342,6 +326,8 @@
 
     lax.fori_loop(0, 2, interior, 0)
     relay_first(0)
+    for unit in range(4):
+        to_twin(unit, (OWN,))
     lax.fori_loop(2, 4, interior, 0)
 
     relay_first(1)
@@ -356,6 +342,7 @@
     for w in (38, 39, 0, 1):
         window(w, True)
 
+    relay_first(3)
     relay_first(2)
     for copy in small_in:
         copy.wait()
@@ -376,6 +363,7 @@
         go(sb.at[0, c], x_recv.at[0, c], left_device, rb.at[0, c])
         go(sb.at[1, c], x_recv.at[1, c], right_device, rb.at[1, c])
     relay_second(1)
+    relay_second(3)
     for c in range(CHUNKS):
         own_sum[:, c * CHUNK : (c + 1) * CHUNK] = mm(oh[TOK : 2 * TOK, :], lf[c])
 
@@ -398,7 +386,7 @@
     relay_second(2)
     lax.fori_loop(4, 8, pair_bias, 0)
     relay_third(0)
-    relay_keys()
+    relay_third(3)
     half = TOK // 2
     first_key = iota((half, WIDTH), 1) < KEYS
     for g in range(HEADS // 2):
@@ -409,8 +397,7 @@
         tb[half:TOK, columns] = jnp.where(first_key, pltpu.roll(even, KEYS, 1), odd).astype(BF16)
 
     relay_third(1)
-    for piece in range(8):
-        await_copy(k_ref(piece, 1 - core), kt_recv.at[piece])
+    arrive(3)
     gathered = kv[...].astype(F32)
     for g in range(2):
         keys = gathered[:, 8 * g : 8 * g + 4, :].reshape(KEYS, HALF).astype(BF16)
@@ -509,10 +496,8 @@
             dma((17,)),
             dma((80,)),
             dma((2,)),
-            dma((8, 3,)),
-            dma((8, 3,)),
-            dma((8,)),
-            dma((8,)),
+            dma((8, 4)),
+            dma((8, 4)),
             dma((2, CHUNKS)),
         ],
         compiler_params=pltpu.CompilerParams(

time: 37.3 us -> 36.5 us (0.979)
  Pallas kernels: 36.5 us -> 35.7 us
    pallas_call x1, Pallas kernels: 35.7 us -> 34.9 us  [call(): pl.pallas_call(functools.partial(kernel, comm), out_shape=(v((ROWS, WIDTH...]
where the time goes in v4:
time: 36.5 us; the launch traced here: 36.4 us
  Pallas kernels  35.7 us (98%)
  between operations  0.64 us (2%)
    pallas_call x1, Pallas kernels, call(): pl.pallas_call(functools.partial(kernel, comm), out_shape=(v((ROWS, WIDTH...  34.9 us
    pallas_call x1, Pallas kernels, write(): pl.pallas_call(write_kernel, out_shape=(jax.ShapeDtypeStruct((ROWS, WIDTH...  0.8 us

profile of v4, /device:TPU:1, one launch (start us, length us, event | category | flops | bytes accessed | tf_op | source)
XLA Modules:
  0.0 36.4 jit_solution(773783516307846319)
XLA Ops:
  0.6 34.9 %shard_map.158 = (bf16[1280,128]{1,0:T(8,128)(2,1)S(1)}, bf16[128,768]{1,0:T(8,128)(2,1)S(1)}) custom-call(bf16[1280,128]{1,0:T(8,128)(2,1)} %atoms_hbm.1, bf16[5120,128]{1,0:T(8,128)(2,1)} %bitcast.7, s32[10,128]{1,0:T(8,128)} %bitcast.9, s32[1,128]{1,0:T(1,128)} %bitcast.12, bf16[128,768]{1,0:T(8,128)(2,1)} %single_hbm.1, bf16[2,4,768]{2,1,0:T(4,128)(2,1)} %kv_hbm.1, ...), custom_call_target="tpu_custom_call" | custom-call | tf_op jit(solution)/shard_map/pallas_call | solution.py:458
  35.6 0.8 %shard_map.159 = (bf16[1280,128]{1,0:T(8,128)(2,1)}, bf16[128,768]{1,0:T(8,128)(2,1)}) custom-call(bf16[1280,128]{1,0:T(8,128)(2,1)S(1)} %get-tuple-element.4.up, bf16[128,768]{1,0:T(8,128)(2,1)S(1)} %get-tuple-element.5.tu), custom_call_target="tpu_custom_call" | custom-call | tf_op jit(solution)/shard_map/pallas_call | solution.py:524
